TPU v7x, 32 devices: a whole 2x2x4 slice. The times are simulated.
32 devices in a mesh: seq: 4 (over y, x), req: 8 (over z, core).
Axes of the slice: x: 2, y: 2, z: 4, core: 2. Of those that a mesh axis runs over, the one named last changes fastest.
Arguments:
- stream_tokens: bfloat16 [16384, 2048], P(('seq', 'req')), may hold values from -6 to 6
- xbc_weight: bfloat16 [2048, 5120], P(None, ('seq', 'req')), may hold values from -0.125 to 0.125
- step_weight: bfloat16 [2048, 64], replicated, may hold values from -0.125 to 0.125
- conv_weight: float32 [4, 5120], replicated, may hold values from -3 to 3
- conv_bias: float32 [5120], replicated, may hold values from -3 to 3
- step_bias: float32 [64], replicated, may hold values from -6 to -4
- decay_rate: float32 [64], replicated, may hold values from 0.02 to 3
- skip_gain: float32 [64], replicated, may hold values from 0.1 to 0.5
- norm_gain: float32 [4096], replicated, may hold values from 0.5 to 1.5
- segment_ids: int32 [8, 2048], P('req'), may hold values from 0 to 1, never falling along the last dimension, each value on 1 to 1536 neighbouring positions
- page_target: int32 [32, 8], P(('seq', 'req')), may hold values from 0 to 7, each once within a row
Outputs:
- mixer_out: bfloat16 [16384, 4096], P(('seq', 'req'))
Inputs may be any that keep to these rules, and one draw needn't show every extreme that they name: `segment_ids`: along each row the ids never fall; each request holds 512 to 1536 consecutive tokens. `page_target`: each row holds every request group's index once.
All inputs are finite; a program needn't handle non-finite values.
Results may differ from a plain program's by a relative error of at most 0.0066.
Values may be sent and summed in bfloat16 or wider, within the bound.
A program may use at most 128 MiB of HBM per device.

v0:
```python
from functools import partial

import jax
import jax.numpy as jnp
from jax import lax
from jax.sharding import PartitionSpec as P

HEADS = 64
HEAD_DIM = 64
GROUPS = 4
STATE = 128
KCONV = 4
SPAN = 256
INNER = 4096
XBC = 5120


def shifted(shard, axis, by):
    peers = lax.axis_size(axis)
    pairs = [(i, i + by) for i in range(peers) if 0 <= i + by < peers]
    return lax.ppermute(shard, axis, pairs)


def conv_rows(raw_rows, seg_rows, prev_raw, prev_seg, conv_weight, conv_bias):
    conv_taps = conv_weight.shape[0]
    row_count = raw_rows.shape[0]
    stacked = jnp.concatenate([prev_raw, raw_rows], axis=0).astype(jnp.float32)
    labels = jnp.concatenate([prev_seg, seg_rows], axis=0)
    summed = conv_bias[None, :] + conv_weight[conv_taps - 1][None, :] * stacked[conv_taps - 1 :]
    for offset in range(conv_taps - 1):
        matching = (labels[offset : offset + row_count] == seg_rows).astype(jnp.float32)
        summed = (
            summed
            + conv_weight[offset][None, :]
            * stacked[offset : offset + row_count]
            * matching[:, None]
        )
    return jax.nn.silu(summed).astype(jnp.bfloat16)


def state_readout(c_mat, state_four):
    upper = state_four.astype(jnp.bfloat16)
    lower = (state_four - upper.astype(jnp.float32)).astype(jnp.bfloat16)
    first = jnp.einsum("tgn,ghpn->tghp", c_mat, upper, preferred_element_type=jnp.float32)
    second = jnp.einsum("tgn,ghpn->tghp", c_mat, lower, preferred_element_type=jnp.float32)
    return first + second


def span_step(decay_rate, state, pieces):
    x_heads, b_mat, c_mat, step_size, seg_rows, seg_before = pieces
    span_len, head_count, head_dim = x_heads.shape
    group_count, state_dim = (b_mat.shape[1], b_mat.shape[2])
    per_group = head_count // group_count
    log_decay = jnp.cumsum(-step_size * decay_rate[None, :], axis=0)
    places = jnp.arange(span_len)
    allowed = (seg_rows[:, None] == seg_rows[None, :]) & (places[:, None] >= places[None, :])
    scores = jnp.einsum("tgn,ugn->gtu", c_mat, b_mat, preferred_element_type=jnp.float32)
    spread = log_decay.T[:, :, None] - log_decay.T[:, None, :]
    decays = jnp.where(allowed[None], jnp.exp(jnp.where(allowed[None], spread, 0.0)), 0.0)
    mixing = (
        scores.reshape(group_count, 1, span_len, span_len)
        * decays.reshape(group_count, per_group, span_len, span_len)
        * step_size.T.reshape(group_count, per_group, 1, span_len)
    ).astype(jnp.bfloat16)
    inside = jnp.einsum(
        "ghtu,ughp->tghp",
        mixing,
        x_heads.reshape(span_len, group_count, per_group, head_dim),
        preferred_element_type=jnp.float32,
    )
    keeping = (seg_rows == seg_before).astype(jnp.float32)
    readout = state_readout(c_mat, state.reshape(group_count, per_group, head_dim, state_dim))
    carried = readout * (keeping[:, None] * jnp.exp(log_decay)).reshape(
        span_len, group_count, per_group, 1
    )
    final_seg = seg_rows[span_len - 1]
    tail_weight = (
        jnp.where(
            seg_rows[:, None] == final_seg,
            jnp.exp(log_decay[span_len - 1][None, :] - log_decay),
            0.0,
        )
        * step_size
    )
    weighted = (x_heads.astype(jnp.float32) * tail_weight[:, :, None]).astype(jnp.bfloat16)
    gained = jnp.einsum(
        "ughp,ugn->ghpn",
        weighted.reshape(span_len, group_count, per_group, head_dim),
        b_mat,
        preferred_element_type=jnp.float32,
    )
    passing = jnp.where(final_seg == seg_before, jnp.exp(log_decay[span_len - 1]), 0.0)
    new_state = passing[:, None, None] * state + gained.reshape(head_count, head_dim, state_dim)
    return (new_state, (inside + carried).reshape(span_len, head_count * head_dim))


def normalize(mixed_rows, x_heads, skip_gain, norm_gain):
    combined = mixed_rows + (x_heads.astype(jnp.float32) * skip_gain[None, :, None]).reshape(
        mixed_rows.shape
    )
    power = jnp.mean(combined * combined, axis=-1, keepdims=True)
    return (combined * lax.rsqrt(power + 1e-05) * norm_gain[None, :]).astype(jnp.bfloat16)


def per_device(
    stream_tokens,
    xbc_weight,
    step_weight,
    conv_weight,
    conv_bias,
    step_bias,
    decay_rate,
    skip_gain,
    norm_gain,
    segment_ids,
    page_target,
):
    req_count = lax.axis_size("req")
    tok_rows = stream_tokens.shape[0]
    page_rows = tok_rows // req_count
    targets = page_target[0]
    page_order = jnp.argsort(targets)
    per_group = HEADS // GROUPS

    def outgoing(values):
        return jnp.take(values.reshape(req_count, page_rows, values.shape[1]), page_order, axis=0)

    raw_rows = jnp.dot(
        stream_tokens,
        lax.all_gather(xbc_weight, ("seq", "req"), axis=1, tiled=True),
        preferred_element_type=jnp.float32,
    ).astype(jnp.bfloat16)
    step_raw = jnp.dot(stream_tokens, step_weight, preferred_element_type=jnp.float32).astype(
        jnp.bfloat16
    )
    raw_rows, step_raw = (raw_rows, step_raw)
    raw_in, step_in = (
        lax.all_to_all(outgoing(raw_rows), "req", split_axis=0, concat_axis=0, tiled=True),
        lax.all_to_all(outgoing(step_raw), "req", split_axis=0, concat_axis=0, tiled=True),
    )
    raw_rows = raw_in.reshape(tok_rows, XBC)
    step_raw = step_in.reshape(tok_rows, HEADS)
    seq_at = lax.axis_index("seq")
    full_ids = segment_ids[0]
    padded_ids = jnp.concatenate([jnp.full((KCONV - 1,), -1, jnp.int32), full_ids])
    seg_rows = lax.dynamic_slice_in_dim(full_ids, seq_at * tok_rows, tok_rows)
    prev_ids = lax.dynamic_slice_in_dim(padded_ids, seq_at * tok_rows, KCONV - 1)
    seg_before = prev_ids[KCONV - 2]
    prev_raw = shifted(raw_rows[tok_rows - (KCONV - 1) :], "seq", 1)
    conv_out = conv_rows(raw_rows, seg_rows, prev_raw, prev_ids, conv_weight, conv_bias)
    step_size = jax.nn.softplus(step_raw.astype(jnp.float32) + step_bias[None, :])
    x_heads = conv_out[:, :INNER].reshape(tok_rows, HEADS, HEAD_DIM)
    b_mat = conv_out[:, INNER : INNER + GROUPS * STATE].reshape(tok_rows, GROUPS, STATE)
    c_mat = conv_out[:, INNER + GROUPS * STATE :].reshape(tok_rows, GROUPS, STATE)
    blocks = tok_rows // SPAN
    block_ends = seg_rows.reshape(blocks, SPAN)[:, SPAN - 1]
    before = jnp.concatenate([seg_before[None], block_ends[:-1]])
    pieces = (
        x_heads.reshape(blocks, SPAN, HEADS, HEAD_DIM),
        b_mat.reshape(blocks, SPAN, GROUPS, STATE),
        c_mat.reshape(blocks, SPAN, GROUPS, STATE),
        step_size.reshape(blocks, SPAN, HEADS),
        seg_rows.reshape(blocks, SPAN),
        before,
    )
    local_state, outputs = lax.scan(
        partial(span_step, decay_rate), jnp.zeros((HEADS, HEAD_DIM, STATE), jnp.float32), pieces
    )
    log_decay = jnp.cumsum(-step_size * decay_rate[None, :], axis=0)
    through = jnp.where(seg_rows[tok_rows - 1] == seg_before, jnp.exp(log_decay[tok_rows - 1]), 0.0)
    incoming = jnp.zeros((HEADS, HEAD_DIM, STATE), jnp.float32)
    for relay_turn in range(lax.axis_size("seq") - 1):
        incoming = shifted(
            (through[:, None, None] * incoming + local_state).astype(jnp.bfloat16), "seq", 1
        ).astype(jnp.float32)
    readout = state_readout(c_mat, incoming.reshape(GROUPS, per_group, HEAD_DIM, STATE))
    keeping = (seg_rows == seg_before).astype(jnp.float32)
    factor = keeping[:, None] * jnp.exp(log_decay)
    mixed_rows = outputs.reshape(tok_rows, INNER) + (
        readout * factor.reshape(tok_rows, GROUPS, per_group, 1)
    ).reshape(tok_rows, INNER)
    normed = normalize(mixed_rows, x_heads, skip_gain, norm_gain)
    returned = lax.all_to_all(
        normed.reshape(req_count, page_rows, INNER), "req", split_axis=0, concat_axis=0, tiled=True
    )
    return jnp.take(returned, targets, axis=0).reshape(tok_rows, INNER)


def solution(mesh):
    in_specs = (
        P(("seq", "req"), None),
        P(None, ("seq", "req")),
        P(),
        P(),
        P(),
        P(),
        P(),
        P(),
        P(),
        P("req", None),
        P(("seq", "req"), None),
    )
    out_specs = P(("seq", "req"), None)
    return jax.shard_map(
        per_device, mesh=mesh, in_specs=in_specs, out_specs=out_specs, check_vma=False
    )
```

profile of v0, /device:TPU:0, one launch (start us, length us, event | category | flops | bytes accessed | tf_op | source)
XLA Modules:
  0.0 646.1 jit_solution(10455791137915560611)
XLA Ops:
  7.3 0.9 copy-done
  8.1 1.7 convolution_convert_fusion.1
  10.0 1.6 sort.17
  12.2 1.3 compare_and_fusion
  13.5 0.8 reshape.325
  14.3 6.3 all-to-all-start
  20.6 127.2 %all-gather.2.cloned.1.call-done = bf16[2048,5120]{0,1:T(8,128)(2,1)} async-done(((bf16[2048,160]{0,1:T(8,128)(2,1)}), bf16[2048,5120]{0,1:T(8,128)(2,1)}) %all-gather.2.cloned.1.call-update) | async-done | bytes 20971536 | tf_op jit(solution)/shard_map/all_gather | solution.py:130
  147.8 16.7 %convolution_convert_fusion = bf16[512,5120]{1,0:T(8,128)(2,1)} fusion(bf16[512,2048]{1,0:T(8,128)(2,1)S(1)} %copy-done, bf16[2048,5120]{0,1:T(8,128)(2,1)} %all-gather.2.cloned.1.call-done), kind=kOutput, calls=%fused_computation.74 | convolution fusion | flops 10740039680 | bytes 28311552 | tf_op jit(solution)/shard_map/dot_general | solution.py:128
  164.6 5.7 gather_fusion.1
  170.2 5.3 broadcast_select_fusion.2
  175.6 4.9 all-to-all-start.1
  184.7 1.4 pad_add_fusion.1
  186.1 1.2 fusion.44
  188.0 1.2 reduce-window.16
  189.9 107.0 %all-to-all-done.1 = bf16[8,64,5120]{2,1,0:T(8,128)(2,1)} async-done(((bf16[8,64,5120]{2,1,0:T(8,128)(2,1)}), bf16[8,64,5120]{2,1,0:T(8,128)(2,1)}, u32[]{:S(2)}, u32[]{:S(2)}) %all-to-all-start.1) | async-done | bytes 5242912 | tf_op jit(solution)/shard_map/all_to_all | solution.py:138
  296.9 0.9 slice.118
  297.8 3.5 collective-permute-start
  301.9 0.9 collective-permute-done
  302.8 4.0 maximum_convert_fusion
  306.9 8.3 %multiply_convert_fusion.6 = bf16[512,5120]{1,0:T(8,128)(2,1)S(1)} fusion(f32[515,5120]{1,0:T(8,128)S(1)} %maximum_convert_fusion, f32[512]{0:T(512)S(1)} %get-tuple-element.154, f32[5120]{0:T(1024)S(1)} %bitcast.221, f32[512]{0:T(512)S(1)} %get-tuple-element.155, f32[5120]{0:T(1024)S(1)} %bitcast.222, f32[512]{0:T(512)S(1)} %get-tuple-element.153, ...), kind=kLoop, calls=%fused_computation.68 | loop fusion | flops 41943040 | bytes 47294464 | tf_op jit(solution)/shard_map/convert_element_type | solution.py:38
  315.2 2.6 slice.123
  317.8 1.0 copy-done.5
  318.9 12.8 %reshape.309 = bf16[2,256,64,64]{3,2,1,0:T(8,128)(2,1)} reshape(bf16[512,4096]{1,0:T(8,128)(2,1)} %slice.123) | data formatting | bytes 8388608 | tf_op jit(solution)/shard_map/reshape;reshape | solution.py:159
  331.7 10.5 %copy.43 = bf16[2,256,64,64]{1,3,2,0:T(8,128)(2,1)} copy(bf16[2,256,64,64]{3,2,1,0:T(8,128)(2,1)} %reshape.309) | data formatting | bytes 8388608
  342.4 76.9 %while.13 = (s32[]{:T(128)}, f32[64,64,128]{2,1,0:T(8,128)}, f32[2,256,4096]{2,1,0:T(8,128)}, s32[2,256]{1,0:T(2,128)S(1)}, s32[2]{0:T(128)S(1)}, /*index=5*/f32...) while((s32[]{:T(128)}, f32[64,64,128]{2,1,0:T(8,128)}, ...), condition=%wide.region_4.5_spmd.clone, body=%wide.region_1.0_spmd.clone.sunk | while | flops 1447363584 | bytes 79509296 | solution.py:166
  343.8 1.2 compare_convert_fusion.3
  346.6 1.8 constant_dynamic-slice_fusion.12
  348.4 2.1 fusion.89
  351.8 3.2 bitcast_add_fusion.4
  355.0 2.7 fusion.91
  357.7 2.6 fusion.90
  361.0 9.3 %fusion.94 = f32[256,4,16,64]{0,3,2,1:T(8,128)} fusion(f32[4,16,64,256]{3,2,1,0:T(8,128)} %fusion.90, f32[4,256,16,64]{1,3,2,0:T(8,128)} %fusion.91, bf16[256,4,16,64]{0,3,2,1:T(8,128)(2,1)} %bitcast.198, f32[4,16,256]{2,1,0:T(8,128)S(1)} %bitcast.205, f32[4,16,256]{2,1,0:T(8,128)S(1)} %reduce_window_sum.61, f32[4,256,256]{2,1,0:T(8,128)S(1)} %fusion.92, ...), kind=kOutput, calls=%fused_computation.13.clone.1 | convolution fusion | flops 565182464 | bytes 15990784 | tf_op jit(solution)/shard_map/while/body/eval_jaxpr/ghtu,ughp->tghp/dot_general | solution.py:65
  370.3 5.6 copy.126
  375.9 4.7 constant_dynamic-update-slice_fusion.2
  380.6 0.8 dynamic-slice.5
  382.0 1.2 compare_convert_fusion.3
  384.7 1.8 constant_dynamic-slice_fusion.12
  386.6 2.1 fusion.89
  390.0 3.9 bitcast_add_fusion.4
  393.8 2.7 fusion.91
  396.5 2.6 fusion.90
  399.8 9.3 %fusion.94 = f32[256,4,16,64]{0,3,2,1:T(8,128)} fusion(f32[4,16,64,256]{3,2,1,0:T(8,128)} %fusion.90, f32[4,256,16,64]{1,3,2,0:T(8,128)} %fusion.91, bf16[256,4,16,64]{0,3,2,1:T(8,128)(2,1)} %bitcast.198, f32[4,16,256]{2,1,0:T(8,128)S(1)} %bitcast.205, f32[4,16,256]{2,1,0:T(8,128)S(1)} %reduce_window_sum.61, f32[4,256,256]{2,1,0:T(8,128)S(1)} %fusion.92, ...), kind=kOutput, calls=%fused_computation.13.clone.1 | convolution fusion | flops 565182464 | bytes 15990784 | tf_op jit(solution)/shard_map/while/body/eval_jaxpr/ghtu,ughp->tghp/dot_general | solution.py:65
  409.0 5.6 copy.126
  414.7 4.7 constant_dynamic-update-slice_fusion.2
  419.4 2.0 add_convert_fusion.2
  421.4 4.5 collective-permute-start.1
  425.9 20.8 %collective-permute-done.1 = bf16[64,64,128]{2,1,0:T(8,128)(2,1)S(1)} collective-permute-done((bf16[64,64,128]{2,1,0:T(8,128)(2,1)S(1)}, bf16[64,64,128]{2,1,0:T(8,128)(2,1)S(1)}, u32[]{:S(2)}, u32[]{:S(2)}) %collective-permute-start.1) | collective-permute-done | bytes 1048608 | tf_op jit(solution)/shard_map/ppermute | solution.py:21
  446.7 1.9 add_convert_fusion.1
  448.6 4.5 collective-permute-start.2
  453.1 20.1 %collective-permute-done.2 = bf16[64,64,128]{2,1,0:T(8,128)(2,1)S(1)} collective-permute-done((bf16[64,64,128]{2,1,0:T(8,128)(2,1)S(1)}, bf16[64,64,128]{2,1,0:T(8,128)(2,1)S(1)}, u32[]{:S(2)}, u32[]{:S(2)}) %collective-permute-start.2) | collective-permute-done | bytes 1048608 | tf_op jit(solution)/shard_map/ppermute | solution.py:21
  473.1 1.3 add_convert_fusion
  474.5 5.3 collective-permute-start.3
  480.2 18.9 %collective-permute-done.3 = bf16[64,64,128]{2,1,0:T(8,128)(2,1)S(1)} collective-permute-done((bf16[64,64,128]{2,1,0:T(8,128)(2,1)}, bf16[64,64,128]{2,1,0:T(8,128)(2,1)S(1)}, u32[]{:S(2)}, u32[]{:S(2)}) %collective-permute-start.3) | collective-permute-done | bytes 1048608 | tf_op jit(solution)/shard_map/ppermute | solution.py:21
  499.2 1.2 fusion.38
  500.4 4.6 bitcast_multiply_fusion.1
  505.0 9.1 %copy.53 = f32[512,4096]{1,0:T(8,128)} copy(f32[512,4096]{0,1:T(8,128)} %bitcast.202) | data formatting | bytes 16777216 | tf_op jit(solution)/shard_map/reshape | solution.py:181
  514.1 8.1 %multiply_reduce_fusion = f32[512]{0:T(512)S(1)} fusion(f32[4096]{0:T(1024)S(1)} %mul.252, f32[512,4096]{1,0:T(8,128)} %copy.53, f32[2,256,4096]{2,1,0:T(8,128)} %get-tuple-element.60, bf16[512,5120]{1,0:T(8,128)(2,1)} %copy-done.5), kind=kLoop, calls=%fused_computation.73 | loop fusion | flops 12582400 | bytes 20989952 | tf_op jit(solution)/shard_map/reduce_sum | solution.py:101
  522.2 1.3 copy-done.4
  523.5 1.2 slice-done.1
  524.7 6.1 multiply_convert_fusion.7
  530.8 4.7 all-to-all-start.2
  535.7 93.8 %all-to-all-done.2 = bf16[8,64,4096]{2,1,0:T(8,128)(2,1)} async-done(((bf16[8,64,4096]{2,1,0:T(8,128)(2,1)}), bf16[8,64,4096]{2,1,0:T(8,128)(2,1)}, u32[]{:S(2)}, u32[]{:S(2)}) %all-to-all-start.2) | async-done | bytes 4194336 | tf_op jit(solution)/shard_map/all_to_all | solution.py:183
  629.5 5.1 gather_fusion.2
  634.6 4.6 bitcast_select_fusion
  (142 shorter events, 13.6 us)
Async XLA Ops:
  6.5 1.6 copy-start
  6.5 141.3 %all-gather.2.cloned.1.call-start = ((), (), s32[]{:S(2)}) async-start(), calls=%async_computation.3 | async-start | bytes 21626880 | tf_op jit(solution)/shard_map/all_gather | solution.py:130
  14.3 161.2 %all-to-all-start = ((bf16[8,2,2048]{2,1,0:T(2,128)(2,1)}), bf16[8,2,2048]{2,1,0:T(2,128)(2,1)S(1)}, u32[]{:S(2)}, u32[]{:S(2)}) async-start(bf16[8,2,2048]{2,1,0:T(2,128)(2,1)} %reshape.325), calls=%async_computation | async-start | bytes 131072 | tf_op jit(solution)/shard_map/all_to_all | solution.py:139
  175.5 4.9 copy-start.18
  175.5 11.8 %copy-start.12 = (f32[4,5120]{1,0:T(4,128)S(1)}, f32[4,5120]{1,0:T(4,128)}, u32[]{:S(2)}) copy-start(f32[4,5120]{1,0:T(4,128)} %param.16) | copy-start | bytes 245764
  175.5 12.3 %copy-start.14 = (f32[64]{0:T(128)S(1)}, f32[64]{0:T(128)}, u32[]{:S(2)}) copy-start(f32[64]{0:T(128)} %param.19) | copy-start | bytes 772
  175.5 12.3 %copy-start.22 = (f32[64]{0:T(128)S(1)}, f32[64]{0:T(128)}, u32[]{:S(2)}) copy-start(f32[64]{0:T(128)} %param.18) | copy-start | bytes 772
  175.6 121.3 %all-to-all-start.1 = ((bf16[8,64,5120]{2,1,0:T(8,128)(2,1)}), bf16[8,64,5120]{2,1,0:T(8,128)(2,1)}, u32[]{:S(2)}, u32[]{:S(2)}) async-start(bf16[8,64,5120]{2,1,0:T(8,128)(2,1)} %broadcast_select_fusion.2), calls=%async_computation.1 | async-start | bytes 10485760 | tf_op jit(solution)/shard_map/all_to_all | solution.py:138
  189.2 117.6 %copy-start.10 = (f32[64,4,128]{2,0,1:T(8,128)}, f32[64,4,128]{2,0,1:T(8,128)S(1)}, u32[]{:S(2)}) copy-start(f32[64,4,128]{2,0,1:T(8,128)S(1)} %reduce-window.16) | copy-start | bytes 393220
  189.5 107.5 %copy-start.15 = (f32[64,4]{0,1:T(4,128)}, f32[64,4]{0,1:T(4,128)S(1)}, u32[]{:S(2)}) copy-start(f32[64,4]{0,1:T(4,128)S(1)} %slice.103) | copy-start | bytes 3076
  189.8 111.6 %copy-start.20 = (f32[64]{0:T(128)}, f32[64]{0:T(128)S(1)}, u32[]{:S(2)}) copy-start(f32[64]{0:T(128)S(1)} %fusion.43) | copy-start | bytes 772
  297.8 5.0 collective-permute-start
  301.9 4.9 copy-start.13
  315.2 3.6 copy-start.5
  318.9 23.4 %copy-start.8 = (bf16[512,512]{1,0:T(8,128)(2,1)}, bf16[512,512]{1,0:T(8,128)(2,1)S(1)}, u32[]{:S(2)}) copy-start(bf16[512,512]{1,0:T(8,128)(2,1)S(1)} %get-tuple-element.148) | copy-start | bytes 1572868
  342.4 77.0 %copy-start.26 = (f32[64]{0:T(128)S(1)}, f32[64]{0:T(128)}, u32[]{:S(2)}) copy-start(f32[64]{0:T(128)} %broadcast_multiply_fusion) | copy-start | bytes 772
  342.4 104.3 %copy-start.21 = (f32[64]{0:T(128)S(1)}, f32[64]{0:T(128)}, u32[]{:S(2)}) copy-start(f32[64]{0:T(128)} %copy-done.20) | copy-start | bytes 772
  342.4 4.1 copy-start.6
  348.4 3.4 copy-start.2
  375.9 4.7 copy-start.7
  380.6 4.1 copy-start.6
  386.6 3.4 copy-start.2
  414.7 4.7 copy-start.7
  419.4 53.8 %copy-start.3 = (f32[64,64,128]{2,1,0:T(8,128)S(1)}, f32[64,64,128]{2,1,0:T(8,128)}, u32[]{:S(2)}) copy-start(f32[64,64,128]{2,1,0:T(8,128)} %get-tuple-element.61) | copy-start | bytes 6291460
  419.4 60.4 %copy-start.23 = (f32[64]{0:T(128)S(1)}, f32[64]{0:T(128)}, u32[]{:S(2)}) copy-start(f32[64]{0:T(128)} %param.20) | copy-start | bytes 772
  419.4 60.5 %copy-start.11 = (f32[64,4,128]{2,0,1:T(8,128)S(1)}, f32[64,4,128]{2,0,1:T(8,128)}, u32[]{:S(2)}) copy-start(f32[64,4,128]{2,0,1:T(8,128)} %copy-done.10) | copy-start | bytes 393220
  419.4 60.5 %copy-start.16 = (f32[64,4]{0,1:T(4,128)S(1)}, f32[64,4]{0,1:T(4,128)}, u32[]{:S(2)}) copy-start(f32[64,4]{0,1:T(4,128)} %copy-done.15) | copy-start | bytes 3076
  419.4 60.5 %copy-start.19 = (f32[512]{0:T(512)S(1)}, f32[512]{0:T(512)}, u32[]{:S(2)}) copy-start(f32[512]{0:T(512)} %get-tuple-element.156) | copy-start | bytes 6148
  419.4 60.6 %copy-start.9 = (bf16[512,512]{1,0:T(8,128)(2,1)S(1)}, bf16[512,512]{1,0:T(8,128)(2,1)}, u32[]{:S(2)}) copy-start(bf16[512,512]{1,0:T(8,128)(2,1)} %copy-done.8) | copy-start | bytes 1572868
  421.4 25.3 %collective-permute-start.1 = (bf16[64,64,128]{2,1,0:T(8,128)(2,1)S(1)}, bf16[64,64,128]{2,1,0:T(8,128)(2,1)S(1)}, u32[]{:S(2)}, u32[]{:S(2)}) collective-permute-start(bf16[64,64,128]{2,1,0:T(8,128)(2,1)S(1)} %add_convert_fusion.2), channel_id=1, source_target_pairs={{0,8},{8,16},{16,24},{1,9},{9,17},{17,25},{2,10},{10,18},{18,26},{... | collective-permute-start | bytes 3145736 | tf_op jit(solution)/shard_map/ppermute | solution.py:21
  448.6 24.5 %collective-permute-start.2 = (bf16[64,64,128]{2,1,0:T(8,128)(2,1)S(1)}, bf16[64,64,128]{2,1,0:T(8,128)(2,1)S(1)}, u32[]{:S(2)}, u32[]{:S(2)}) collective-permute-start(bf16[64,64,128]{2,1,0:T(8,128)(2,1)S(1)} %add_convert_fusion.1), channel_id=1, source_target_pairs={{0,8},{8,16},{16,24},{1,9},{9,17},{17,25},{2,10},{10,18},{18,26},{... | collective-permute-start | bytes 3145736 | tf_op jit(solution)/shard_map/ppermute | solution.py:21
  474.5 24.7 %collective-permute-start.3 = (bf16[64,64,128]{2,1,0:T(8,128)(2,1)}, bf16[64,64,128]{2,1,0:T(8,128)(2,1)S(1)}, u32[]{:S(2)}, u32[]{:S(2)}) collective-permute-start(bf16[64,64,128]{2,1,0:T(8,128)(2,1)} %add_convert_fusion), channel_id=1, source_target_pairs={{0,8},{8,16},{16,24},{1,9},{9,17},{17,25},{2,10},{10,18},{18,26},{... | collective-permute-start | bytes 3145736 | tf_op jit(solution)/shard_map/ppermute | solution.py:21
  505.0 17.2 %slice-start = ((s8[5242880]{0:T(1024)(128)(4,1)}), s8[1048576]{0:T(1024)(128)(4,1)S(1)}, s32[]{:S(2)}) async-start(s8[5242880]{0:T(1024)(128)(4,1)} %bitcast.200), calls=%async_computation.4 | async-start | bytes 2097152
  514.1 9.4 %copy-start.4 = (f32[512,4096]{1,0:T(8,128)S(1)}, f32[512,4096]{1,0:T(8,128)}, u32[]{:S(2)}) copy-start(f32[512,4096]{1,0:T(8,128)} %copy.53) | copy-start | bytes 25165828
  514.1 10.6 %slice-start.1 = ((s8[5242880]{0:T(1024)(128)(4,1)}), s8[4194304]{0:T(1024)(128)(4,1)S(1)}, s32[]{:S(2)}) async-start(s8[5242880]{0:T(1024)(128)(4,1)} %bitcast.200), calls=%async_computation.5 | async-start | bytes 8388608
  514.1 10.6 %copy-start.17 = (f32[4096]{0:T(1024)S(1)}, f32[4096]{0:T(1024)}, u32[]{:S(2)}) copy-start(f32[4096]{0:T(1024)} %param.21) | copy-start | bytes 49156
  530.8 4.7 copy-start.25
  530.8 4.9 copy-start.24
  530.8 98.7 %all-to-all-start.2 = ((bf16[8,64,4096]{2,1,0:T(8,128)(2,1)}), bf16[8,64,4096]{2,1,0:T(8,128)(2,1)}, u32[]{:S(2)}, u32[]{:S(2)}) async-start(bf16[8,64,4096]{2,1,0:T(8,128)(2,1)} %bitcast.203), calls=%async_computation.2 | async-start | bytes 8388608 | tf_op jit(solution)/shard_map/all_to_all | solution.py:183
  629.5 9.8 %copy-start.1 = (bf16[512,2048]{1,0:T(8,128)(2,1)S(1)}, bf16[512,2048]{1,0:T(8,128)(2,1)}, u32[]{:S(2)}) copy-start(bf16[512,2048]{1,0:T(8,128)(2,1)} %param.13) | copy-start | bytes 6291460
Sparse Core Ops, SparseCore 0:
  10.2 137.5 all-gather.1
where the time goes:
time: 650 us; the launch traced here: 646 us
  waiting for transfers between devices  389 us (60%)
  local copies, waits for them, and re-layouts  85.4 us (13%)
  other arithmetic  61.7 us (9%)
  matrix products  58.2 us (9%)
  starting transfers between devices  33.6 us (5%)
  between operations  15.1 us (2%)
    all_gather x1, waiting for transfers between devices, per_device(): lax.all_gather(xbc_weight, ('seq', 'req'), axis=1, tiled=True)  127 us
    all_to_all x1, waiting for transfers between devices, per_device(): lax.all_to_all(outgoing(raw_rows), 'req', split_axis=0, concat_axis=0, ti...  107 us
    all_to_all x1, waiting for transfers between devices, per_device(): lax.all_to_all(normed.reshape(req_count, page_rows, INNER), 'req', split_...  93.8 us
    ppermute x4, waiting for transfers between devices, shifted(): return lax.ppermute(shard, axis, pairs)  60.6 us
    dynamic_update_slice x4, local copies, waits for them, and re-layouts, per_device(): lax.scan(partial(span_step, decay_rate), jnp.zeros((HEADS, HEAD_DIM, STAT...  20.6 us
    dot_general x2, matrix products, span_step(): jnp.einsum('ghtu,ughp->tghp', mixing, x_heads.reshape(span_len, group_cou...  18.6 us
    ppermute x4, starting transfers between devices, shifted(): return lax.ppermute(shard, axis, pairs)  17.7 us
    dot_general x1, matrix products, per_device(): jnp.dot(stream_tokens, lax.all_gather(xbc_weight, ('seq', 'req'), axis=1,...  16.7 us
  transfers between devices with their start and end apart: 8, of which 7 were waited for; matrix products, arithmetic and copies ran while one was open for 7% of the time, Pallas kernels for 0%

commit v1 on v0

--- a/solution.py
+++ b/solution.py
@@ -102,6 +102,9 @@
     return (combined * lax.rsqrt(power + 1e-05) * norm_gain[None, :]).astype(jnp.bfloat16)
 
 
+HALO = 16
+
+
 def per_device(
     stream_tokens,
     xbc_weight,
@@ -116,37 +119,34 @@
     page_target,
 ):
     req_count = lax.axis_size("req")
+    seq_count = lax.axis_size("seq")
     tok_rows = stream_tokens.shape[0]
     page_rows = tok_rows // req_count
     targets = page_target[0]
-    page_order = jnp.argsort(targets)
+    spots = jnp.arange(req_count, dtype=jnp.int32)
+    page_order = jnp.sum(jnp.where(targets[None, :] == spots[:, None], spots[None, :], 0), axis=1)
     per_group = HEADS // GROUPS
-
-    def outgoing(values):
-        return jnp.take(values.reshape(req_count, page_rows, values.shape[1]), page_order, axis=0)
-
-    raw_rows = jnp.dot(
-        stream_tokens,
-        lax.all_gather(xbc_weight, ("seq", "req"), axis=1, tiled=True),
-        preferred_element_type=jnp.float32,
-    ).astype(jnp.bfloat16)
-    step_raw = jnp.dot(stream_tokens, step_weight, preferred_element_type=jnp.float32).astype(
+    in_bounds = "clip"
+
+    pages = stream_tokens.reshape(req_count, page_rows, stream_tokens.shape[1])
+    outgoing = jnp.take(pages, page_order, axis=0, mode=in_bounds)
+    tokens = lax.all_to_all(outgoing, "req", split_axis=0, concat_axis=0, tiled=True)
+    tokens = tokens.reshape(tok_rows, stream_tokens.shape[1])
+    prev_tokens = shifted(tokens[tok_rows - HALO :], "seq", 1)
+    full_weight = lax.all_gather(xbc_weight, ("seq", "req"), axis=1, tiled=True)
+    all_rows = jnp.concatenate([prev_tokens, tokens], axis=0)
+    raw_all = jnp.dot(all_rows, full_weight, preferred_element_type=jnp.float32).astype(
         jnp.bfloat16
     )
-    raw_rows, step_raw = (raw_rows, step_raw)
-    raw_in, step_in = (
-        lax.all_to_all(outgoing(raw_rows), "req", split_axis=0, concat_axis=0, tiled=True),
-        lax.all_to_all(outgoing(step_raw), "req", split_axis=0, concat_axis=0, tiled=True),
-    )
-    raw_rows = raw_in.reshape(tok_rows, XBC)
-    step_raw = step_in.reshape(tok_rows, HEADS)
+    step_raw = jnp.dot(tokens, step_weight, preferred_element_type=jnp.float32).astype(jnp.bfloat16)
+    prev_raw, raw_rows = (raw_all[HALO - (KCONV - 1) : HALO], raw_all[HALO:])
+
     seq_at = lax.axis_index("seq")
     full_ids = segment_ids[0]
     padded_ids = jnp.concatenate([jnp.full((KCONV - 1,), -1, jnp.int32), full_ids])
     seg_rows = lax.dynamic_slice_in_dim(full_ids, seq_at * tok_rows, tok_rows)
     prev_ids = lax.dynamic_slice_in_dim(padded_ids, seq_at * tok_rows, KCONV - 1)
     seg_before = prev_ids[KCONV - 2]
-    prev_raw = shifted(raw_rows[tok_rows - (KCONV - 1) :], "seq", 1)
     conv_out = conv_rows(raw_rows, seg_rows, prev_raw, prev_ids, conv_weight, conv_bias)
     step_size = jax.nn.softplus(step_raw.astype(jnp.float32) + step_bias[None, :])
     x_heads = conv_out[:, :INNER].reshape(tok_rows, HEADS, HEAD_DIM)
@@ -168,11 +168,14 @@
     )
     log_decay = jnp.cumsum(-step_size * decay_rate[None, :], axis=0)
     through = jnp.where(seg_rows[tok_rows - 1] == seg_before, jnp.exp(log_decay[tok_rows - 1]), 0.0)
+    all_states = lax.all_gather(local_state.astype(jnp.bfloat16), "seq")
+    all_through = lax.all_gather(through, "seq")
     incoming = jnp.zeros((HEADS, HEAD_DIM, STATE), jnp.float32)
-    for relay_turn in range(lax.axis_size("seq") - 1):
-        incoming = shifted(
-            (through[:, None, None] * incoming + local_state).astype(jnp.bfloat16), "seq", 1
-        ).astype(jnp.float32)
+    running = jnp.ones((HEADS,), jnp.float32)
+    for turn in range(seq_count - 2, -1, -1):
+        used = (turn < seq_at).astype(jnp.float32)
+        incoming = incoming + (used * running)[:, None, None] * all_states[turn].astype(jnp.float32)
+        running = jnp.where(turn < seq_at, running * all_through[turn], running)
     readout = state_readout(c_mat, incoming.reshape(GROUPS, per_group, HEAD_DIM, STATE))
     keeping = (seg_rows == seg_before).astype(jnp.float32)
     factor = keeping[:, None] * jnp.exp(log_decay)
@@ -183,7 +186,7 @@
     returned = lax.all_to_all(
         normed.reshape(req_count, page_rows, INNER), "req", split_axis=0, concat_axis=0, tiled=True
     )
-    return jnp.take(returned, targets, axis=0).reshape(tok_rows, INNER)
+    return jnp.take(returned, targets, axis=0, mode=in_bounds).reshape(tok_rows, INNER)
 
 
 def solution(mesh):

time: 650 us -> 512 us (0.79)
  waiting for transfers between devices: 389 us -> 284 us
  starting transfers between devices: 33.6 us -> 14.4 us
  other arithmetic: 61.7 us -> 47.9 us
  blocking collectives: 0 us -> 7.89 us
    ppermute x4 -> x1, waiting for transfers between devices: 60.6 us -> 0.31 us  [shifted(): return lax.ppermute(shard, axis, pairs)]
    all_to_all x2 -> x1, waiting for transfers between devices: 107 us -> 82.6 us  [per_device(): lax.all_to_all(outgoing, 'req', split_axis=0, concat_axis=0, tiled=True)]
    all_gather x1 -> x2, waiting for transfers between devices: 127 us -> 106 us  [the longest x1 67.9 us: per_device(): full_weight = lax.all_gather(xbc_weight, ('seq', 'req'), axis=1, tiled=True)]
    ppermute x4 -> x1, starting transfers between devices: 17.7 us -> 3.34 us  [shifted(): return lax.ppermute(shard, axis, pairs)]
    select_n x6 -> x0, other arithmetic: 10.2 us -> none  [the longest x3 5.41 us: outgoing(): jnp.take(values.reshape(req_count, page_rows, values.shape[1]), page_orde...]
    all_gather x0 -> x1, blocking collectives: none -> 7.89 us  [per_device(): all_through = lax.all_gather(through, 'seq')]
    unnamed x55 -> x39, local copies, waits for them, and re-layouts: 15.8 us -> 14 us
  transfers between devices with their start and end apart: 8 -> 5, of which waited for: 7 -> 5; matrix products, arithmetic and copies ran while one was open for 7% -> 3% of each run, Pallas kernels for 0% -> 0%
where the time goes in v1:
time: 512 us; the launch traced here: 510 us
  waiting for transfers between devices  284 us (55%)
  local copies, waits for them, and re-layouts  80.4 us (16%)
  matrix products  58 us (11%)
  other arithmetic  47.9 us (9%)
  between operations  14.9 us (3%)
  starting transfers between devices  14.4 us (3%)
  blocking collectives  7.89 us (2%)
    all_to_all x1, waiting for transfers between devices, per_device(): lax.all_to_all(normed.reshape(req_count, page_rows, INNER), 'req', split_...  94.1 us
    all_to_all x1, waiting for transfers between devices, per_device(): lax.all_to_all(outgoing, 'req', split_axis=0, concat_axis=0, tiled=True)  82.6 us
    all_gather x1, waiting for transfers between devices, per_device(): full_weight = lax.all_gather(xbc_weight, ('seq', 'req'), axis=1, tiled=True)  67.9 us
    all_gather x1, waiting for transfers between devices, per_device(): all_states = lax.all_gather(local_state.astype(jnp.bfloat16), 'seq')  38.2 us
    dynamic_update_slice x4, local copies, waits for them, and re-layouts, per_device(): lax.scan(partial(span_step, decay_rate), jnp.zeros((HEADS, HEAD_DIM, STAT...  20.6 us
    dot_general x2, matrix products, span_step(): jnp.einsum('ghtu,ughp->tghp', mixing, x_heads.reshape(span_len, group_cou...  18.6 us
    dot_general x1, matrix products, per_device(): jnp.dot(all_rows, full_weight, preferred_element_type=jnp.float32)  17.1 us
    unnamed x39, local copies, waits for them, and re-layouts  14 us
  transfers between devices with their start and end apart: 5, of which 5 were waited for; matrix products, arithmetic and copies ran while one was open for 3% of the time, Pallas kernels for 0%

profile of v1, /device:TPU:0, one launch (start us, length us, event | category | flops | bytes accessed | tf_op | source)
XLA Modules:
  0.0 510.4 jit_solution(3523742377801588544)
XLA Ops:
  6.5 0.7 all-gather.5.cloned.1.call-update
  7.3 0.8 select_reduce_fusion
  8.1 2.0 gather_fusion
  10.1 6.3 %all-to-all-start = ((bf16[8,64,2048]{2,1,0:T(8,128)(2,1)}), bf16[8,64,2048]{2,1,0:T(8,128)(2,1)S(1)}, u32[]{:S(2)}, u32[]{:S(2)}) async-start(bf16[8,64,2048]{2,1,0:T(8,128)(2,1)} %gather_fusion), calls=%async_computation | async-start | bytes 4194304 | tf_op jit(solution)/shard_map/all_to_all | solution.py:133
  16.6 0.6 slice.101
  17.3 0.6 broadcast.179
  17.8 0.6 fusion.69
  18.5 0.6 slice.143
  19.1 1.3 pad_add_fusion.1
  20.5 1.2 fusion.64
  21.8 82.6 %all-to-all-done = bf16[8,64,2048]{2,1,0:T(8,128)(2,1)S(1)} async-done(((bf16[8,64,2048]{2,1,0:T(8,128)(2,1)}), bf16[8,64,2048]{2,1,0:T(8,128)(2,1)S(1)}, u32[]{:S(2)}, u32[]{:S(2)}) %all-to-all-start) | async-done | bytes 2097184 | tf_op jit(solution)/shard_map/all_to_all | solution.py:133
  104.4 3.3 collective-permute-start
  107.8 1.5 compare_select_fusion.1
  109.4 0.3 collective-permute-done
  109.7 67.9 %all-gather.5.cloned.1.call-done = bf16[2048,5120]{0,1:T(8,128)(2,1)} async-done(((bf16[2048,160]{0,1:T(8,128)(2,1)}), bf16[2048,5120]{0,1:T(8,128)(2,1)}) %all-gather.5.cloned.1.call-update) | async-done | bytes 20971536 | tf_op jit(solution)/shard_map/all_gather | solution.py:136
  177.5 17.1 %fusion.39 = bf16[528,5120]{1,0:T(8,128)(2,1)} fusion(bf16[2048,5120]{0,1:T(8,128)(2,1)} %all-gather.5.cloned.1.call-done, bf16[512,2048]{1,0:T(8,128)(2,1)S(1)} %bitcast.220, bf16[16,2048]{1,0:T(8,128)(2,1)S(1)} %collective-permute-done), kind=kOutput, calls=%fused_computation.75 | convolution fusion | flops 11077287936 | bytes 28540928 | tf_op jit(solution)/shard_map/dot_general | solution.py:138
  194.7 4.0 fusion.38
  198.7 8.3 %multiply_convert_fusion.6 = bf16[512,5120]{1,0:T(8,128)(2,1)S(1)} fusion(f32[515,5120]{1,0:T(8,128)S(1)} %fusion.38, f32[512]{0:T(512)S(1)} %get-tuple-element.184, f32[5120]{0:T(1024)S(1)} %bitcast.231, f32[512]{0:T(512)S(1)} %get-tuple-element.185, f32[5120]{0:T(1024)S(1)} %bitcast.232, f32[512]{0:T(512)S(1)} %get-tuple-element.183, ...), kind=kLoop, calls=%fused_computation.68 | loop fusion | flops 41943040 | bytes 47294464 | tf_op jit(solution)/shard_map/convert_element_type | solution.py:38
  207.0 2.6 slice.149
  209.6 0.9 copy-done.4
  210.7 12.8 %reshape.290 = bf16[2,256,64,64]{3,2,1,0:T(8,128)(2,1)} reshape(bf16[512,4096]{1,0:T(8,128)(2,1)} %slice.149) | data formatting | bytes 8388608 | tf_op jit(solution)/shard_map/reshape;reshape | solution.py:159
  223.4 10.5 %copy.73 = bf16[2,256,64,64]{1,3,2,0:T(8,128)(2,1)} copy(bf16[2,256,64,64]{3,2,1,0:T(8,128)(2,1)} %reshape.290) | data formatting | bytes 8388608
  234.2 77.2 %while.13 = (s32[]{:T(128)}, f32[64,64,128]{2,1,0:T(8,128)}, f32[2,256,4096]{2,1,0:T(8,128)}, s32[2,256]{1,0:T(2,128)S(1)}, s32[2]{0:T(128)S(1)}, /*index=5*/f32...) while((s32[]{:T(128)}, f32[64,64,128]{2,1,0:T(8,128)}, ...), condition=%wide.region_4.5_spmd.clone, body=%wide.region_1.4_spmd.clone.sunk | while | flops 1447363584 | bytes 79574832 | solution.py:166
  234.6 0.6 reduce-window.26
  235.7 0.7 dynamic-slice.5
  236.3 0.6 dynamic_slice.57
  236.9 1.3 compare_convert_fusion.3
  238.6 1.8 constant_dynamic-slice_fusion.12
  240.4 2.1 fusion.108
  243.8 3.2 bitcast_add_fusion.4
  247.0 2.7 fusion.110
  249.7 2.7 fusion.109
  253.0 9.3 %fusion.113 = f32[256,4,16,64]{0,3,2,1:T(8,128)} fusion(f32[4,16,64,256]{3,2,1,0:T(8,128)} %fusion.109, f32[4,256,16,64]{1,3,2,0:T(8,128)} %fusion.110, bf16[256,4,16,64]{0,3,2,1:T(8,128)(2,1)} %bitcast.206, f32[4,16,256]{2,1,0:T(8,128)S(1)} %bitcast.224, f32[4,16,256]{2,1,0:T(8,128)S(1)} %reduce_window_sum.61, f32[4,256,256]{2,1,0:T(8,128)S(1)} %fusion.111, ...), kind=kOutput, calls=%fused_computation.12.clone.1 | convolution fusion | flops 565182464 | bytes 15990784 | tf_op jit(solution)/shard_map/while/body/eval_jaxpr/ghtu,ughp->tghp/dot_general | solution.py:65
  262.3 5.6 %copy.164 = f32[1,256,4096]{2,1,0:T(8,128)} copy(f32[1,256,4096]{1,2,0:T(8,128)} %bitcast.207) | data formatting | bytes 8388608 | tf_op jit(solution)/shard_map/while/body/jit(dynamic_update_index_in_dim)/dynamic_update_slice | solution.py:166
  267.9 4.7 constant_dynamic-update-slice_fusion.2
  272.7 0.6 reduce-window.26
  273.9 0.7 dynamic-slice.5
  274.5 0.6 dynamic_slice.57
  275.1 1.3 compare_convert_fusion.3
  276.8 1.8 constant_dynamic-slice_fusion.12
  278.6 2.1 fusion.108
  282.0 3.8 bitcast_add_fusion.4
  285.9 2.7 fusion.110
  288.5 2.7 fusion.109
  291.8 9.3 %fusion.113 = f32[256,4,16,64]{0,3,2,1:T(8,128)} fusion(f32[4,16,64,256]{3,2,1,0:T(8,128)} %fusion.109, f32[4,256,16,64]{1,3,2,0:T(8,128)} %fusion.110, bf16[256,4,16,64]{0,3,2,1:T(8,128)(2,1)} %bitcast.206, f32[4,16,256]{2,1,0:T(8,128)S(1)} %bitcast.224, f32[4,16,256]{2,1,0:T(8,128)S(1)} %reduce_window_sum.61, f32[4,256,256]{2,1,0:T(8,128)S(1)} %fusion.111, ...), kind=kOutput, calls=%fused_computation.12.clone.1 | convolution fusion | flops 565182464 | bytes 15990784 | tf_op jit(solution)/shard_map/while/body/eval_jaxpr/ghtu,ughp->tghp/dot_general | solution.py:65
  301.1 5.6 %copy.164 = f32[1,256,4096]{2,1,0:T(8,128)} copy(f32[1,256,4096]{1,2,0:T(8,128)} %bitcast.207) | data formatting | bytes 8388608 | tf_op jit(solution)/shard_map/while/body/jit(dynamic_update_index_in_dim)/dynamic_update_slice | solution.py:166
  306.7 4.7 constant_dynamic-update-slice_fusion.2
  311.4 2.8 convert_element_type.118
  314.3 1.3 constant_dynamic-slice_fusion.5
  317.1 1.2 reduce-window.16
  318.8 7.9 %all-gather.1 = f32[4,1,64]{2,1,0:T(1,128)S(1)} all-gather(f32[1,1,64]{2,1,0:T(1,128)S(1)} %bitcast.236), channel_id=1, replica_groups=mesh['seq'=4,'req'=8] {'seq'}, dimensions={0}, use_global_device_ids=true | all-gather | bytes 1280 | tf_op jit(solution)/shard_map/all_gather | solution.py:172
  327.2 38.2 %all-gather.7.cloned.1.call-done = bf16[256,64,128]{2,1,0:T(8,128)(2,1)} async-done(((bf16[64,64,128]{2,1,0:T(8,128)(2,1)}), bf16[256,64,128]{2,1,0:T(8,128)(2,1)}) %all-gather.7.cloned.1.call-update) | async-done | bytes 4194320 | tf_op jit(solution)/shard_map/all_gather | solution.py:171
  365.3 1.7 fusion.71
  367.1 1.5 convert_multiply_fusion.2
  368.6 1.3 fusion.50
  369.9 4.0 bitcast_multiply_fusion.1
  373.9 9.0 %copy.81 = f32[512,4096]{1,0:T(8,128)} copy(f32[512,4096]{0,1:T(8,128)} %bitcast.210) | data formatting | bytes 16777216 | tf_op jit(solution)/shard_map/reshape | solution.py:184
  382.9 8.1 %multiply_reduce_fusion = f32[512]{0:T(512)S(1)} fusion(f32[4096]{0:T(1024)S(1)} %mul.295, f32[512,4096]{1,0:T(8,128)} %copy.81, f32[2,256,4096]{2,1,0:T(8,128)} %get-tuple-element.58, bf16[512,5120]{1,0:T(8,128)(2,1)} %copy-done.4), kind=kLoop, calls=%fused_computation.73 | loop fusion | flops 12582400 | bytes 20989952 | tf_op jit(solution)/shard_map/reduce_sum | solution.py:101
  391.1 1.3 copy-done.3
  392.3 1.2 slice-done.1
  393.5 6.1 %multiply_convert_fusion.7 = bf16[512,4096]{1,0:T(8,128)(2,1)} fusion(f32[4096]{0:T(1024)S(1)} %copy-done.14, f32[512]{0:T(512)S(1)} %add_rsqrt_fusion, f32[4096]{0:T(1024)S(1)} %mul.295, f32[512,4096]{1,0:T(8,128)S(1)} %copy-done.3, f32[2,256,4096]{2,1,0:T(8,128)} %get-tuple-element.58, bf16[512,5120]{1,0:T(8,128)(2,1)S(1)} %bitcast.209), kind=kLoop, calls=%fused_computation.72 | loop fusion | flops 14680064 | bytes 25200640 | tf_op jit(solution)/shard_map/convert_element_type | solution.py:102
  399.7 4.7 all-to-all-start.1
  404.4 94.1 %all-to-all-done.1 = bf16[8,64,4096]{2,1,0:T(8,128)(2,1)} async-done(((bf16[8,64,4096]{2,1,0:T(8,128)(2,1)}), bf16[8,64,4096]{2,1,0:T(8,128)(2,1)}, u32[]{:S(2)}, u32[]{:S(2)}) %all-to-all-start.1) | async-done | bytes 4194336 | tf_op jit(solution)/shard_map/all_to_all | solution.py:186
  498.5 5.0 gather_fusion.1
  (113 shorter events, 5.1 us)
Async XLA Ops:
  6.5 1.6 copy-start
  6.5 171.0 %all-gather.5.cloned.1.call-start = ((), (), s32[]{:S(2)}) async-start(), calls=%async_computation.2 | async-start | bytes 21626880 | tf_op jit(solution)/shard_map/all_gather | solution.py:136
  8.1 8.4 %copy-start.15 = (s32[1,2048]{1,0:T(1,128)S(1)}, s32[1,2048]{1,0:T(1,128)}, u32[]{:S(2)}) copy-start(s32[1,2048]{1,0:T(1,128)} %param.22) | copy-start | bytes 24580
  8.1 13.6 %copy-start.11 = (f32[4,5120]{1,0:T(4,128)S(1)}, f32[4,5120]{1,0:T(4,128)}, u32[]{:S(2)}) copy-start(f32[4,5120]{1,0:T(4,128)} %param.16) | copy-start | bytes 245764
  8.1 99.7 %copy-start.10 = (bf16[2048,64]{0,1:T(8,128)(2,1)S(1)}, bf16[2048,64]{0,1:T(8,128)(2,1)}, u32[]{:S(2)}) copy-start(bf16[2048,64]{0,1:T(8,128)(2,1)} %param.15) | copy-start | bytes 786436
  8.1 99.7 %copy-start.19 = (f32[64]{0:T(128)S(1)}, f32[64]{0:T(128)}, u32[]{:S(2)}) copy-start(f32[64]{0:T(128)} %param.18) | copy-start | bytes 772
  10.1 94.3 %all-to-all-start = ((bf16[8,64,2048]{2,1,0:T(8,128)(2,1)}), bf16[8,64,2048]{2,1,0:T(8,128)(2,1)S(1)}, u32[]{:S(2)}, u32[]{:S(2)}) async-start(bf16[8,64,2048]{2,1,0:T(8,128)(2,1)} %gather_fusion), calls=%async_computation | async-start | bytes 4194304 | tf_op jit(solution)/shard_map/all_to_all | solution.py:133
  16.5 348.9 %all-gather.7.cloned.1.call-start = ((), (), s32[]{:S(2)}) async-start(), calls=%async_computation.3 | async-start | bytes 5242880 | tf_op jit(solution)/shard_map/all_gather | solution.py:171
  104.4 5.2 %collective-permute-start = (bf16[16,2048]{1,0:T(8,128)(2,1)S(1)}, bf16[16,2048]{1,0:T(8,128)(2,1)S(1)}, u32[]{:S(2)}, u32[]{:S(2)}) collective-permute-start(bf16[16,2048]{1,0:T(8,128)(2,1)S(1)} %slice.144), channel_id=1, source_target_pairs={{0,8},{8,16},{16,24},{1,9},{9,17},{17,25},{2,10},{10,18},{18,26},{... | collective-permute-start | bytes 196616 | tf_op jit(solution)/shard_map/ppermute | solution.py:21
  194.7 4.0 copy-start.12
  207.0 3.6 copy-start.4
  210.6 23.4 %copy-start.7 = (bf16[512,512]{1,0:T(8,128)(2,1)}, bf16[512,512]{1,0:T(8,128)(2,1)S(1)}, u32[]{:S(2)}) copy-start(bf16[512,512]{1,0:T(8,128)(2,1)S(1)} %get-tuple-element.175) | copy-start | bytes 1572868
  223.4 10.8 %copy-start.13 = (f32[64]{0:T(128)S(1)}, f32[64]{0:T(128)}, u32[]{:S(2)}) copy-start(f32[64]{0:T(128)} %param.19) | copy-start | bytes 772
  234.4 4.2 copy-start.5
  240.4 3.4 copy-start.2
  267.9 4.7 copy-start.6
  272.6 4.2 copy-start.5
  278.6 3.4 copy-start.2
  306.7 4.7 copy-start.6
  311.4 5.4 %copy-start.17 = (f32[64]{0:T(128)S(1)}, f32[64]{0:T(128)}, u32[]{:S(2)}) copy-start(f32[64]{0:T(128)} %param.20) | copy-start | bytes 772
  311.4 5.6 %copy-start.9 = (f32[512,64]{0,1:T(8,128)S(1)}, f32[512,64]{0,1:T(8,128)}, u32[]{:S(2)}) copy-start(f32[512,64]{0,1:T(8,128)} %get-tuple-element.190) | copy-start | bytes 393220
  311.4 15.5 %copy-start.16 = (f32[512]{0:T(512)S(1)}, f32[512]{0:T(512)}, u32[]{:S(2)}) copy-start(f32[512]{0:T(512)} %get-tuple-element.186) | copy-start | bytes 6148
  311.4 15.6 %copy-start.8 = (bf16[512,512]{1,0:T(8,128)(2,1)S(1)}, bf16[512,512]{1,0:T(8,128)(2,1)}, u32[]{:S(2)}) copy-start(bf16[512,512]{1,0:T(8,128)(2,1)} %copy-done.7) | copy-start | bytes 1572868
  373.9 17.1 %slice-start = ((s8[5242880]{0:T(1024)(128)(4,1)}), s8[1048576]{0:T(1024)(128)(4,1)S(1)}, s32[]{:S(2)}) async-start(s8[5242880]{0:T(1024)(128)(4,1)} %bitcast.208), calls=%async_computation.4 | async-start | bytes 2097152
  382.9 9.4 %copy-start.3 = (f32[512,4096]{1,0:T(8,128)S(1)}, f32[512,4096]{1,0:T(8,128)}, u32[]{:S(2)}) copy-start(f32[512,4096]{1,0:T(8,128)} %copy.81) | copy-start | bytes 25165828
  382.9 10.6 %slice-start.1 = ((s8[5242880]{0:T(1024)(128)(4,1)}), s8[4194304]{0:T(1024)(128)(4,1)S(1)}, s32[]{:S(2)}) async-start(s8[5242880]{0:T(1024)(128)(4,1)} %bitcast.208), calls=%async_computation.5 | async-start | bytes 8388608
  382.9 10.6 %copy-start.14 = (f32[4096]{0:T(1024)S(1)}, f32[4096]{0:T(1024)}, u32[]{:S(2)}) copy-start(f32[4096]{0:T(1024)} %param.21) | copy-start | bytes 49156
  399.7 4.7 copy-start.18
  399.7 98.8 %all-to-all-start.1 = ((bf16[8,64,4096]{2,1,0:T(8,128)(2,1)}), bf16[8,64,4096]{2,1,0:T(8,128)(2,1)}, u32[]{:S(2)}, u32[]{:S(2)}) async-start(bf16[8,64,4096]{2,1,0:T(8,128)(2,1)} %bitcast.213), calls=%async_computation.1 | async-start | bytes 8388608 | tf_op jit(solution)/shard_map/all_to_all | solution.py:186
  404.4 99.1 %copy-start.1 = (bf16[512,2048]{1,0:T(8,128)(2,1)S(1)}, bf16[512,2048]{1,0:T(8,128)(2,1)}, u32[]{:S(2)}) copy-start(bf16[512,2048]{1,0:T(8,128)(2,1)} %param.13) | copy-start | bytes 6291460
Sparse Core Ops, SparseCore 0:
  10.2 167.2 all-gather.4
  314.4 50.8 all-gather.6

commit v2 on v1

v2 whole, which is shorter than its diff:
```python
from functools import partial

import jax
import jax.numpy as jnp
from jax import lax
from jax.experimental import pallas as pl
from jax.experimental.pallas import tpu as pltpu
from jax.sharding import PartitionSpec as P

HEADS = 64
HEAD_DIM = 64
GROUPS = 4
STATE = 128
KCONV = 4
SPAN = 256
INNER = 4096
XBC = 5120


def shifted(shard, axis, by):
    peers = lax.axis_size(axis)
    pairs = [(i, i + by) for i in range(peers) if 0 <= i + by < peers]
    return lax.ppermute(shard, axis, pairs)


HALO = 16
PER_GROUP = HEADS // GROUPS
WIDE = PER_GROUP * HEAD_DIM
LANES = 128
VMEM_LIMIT = 40 * 1024 * 1024


def dot32(left, right, contract=((1,), (0,))):
    return lax.dot_general(left, right, (contract, ((), ())), preferred_element_type=jnp.float32)


def conv_kernel(
    raw_x, raw_b, raw_c, w_x, w_b, w_c, bias_x, bias_b, bias_c, match, tail, pass_last, expand,
    x_out, b_out, c_out, first_state, last_state, wide,
):
    rows = x_out.shape[0]
    piece = 64

    def conv(raw, weight, bias, out):
        wide[:, : raw.shape[1]] = raw[...].astype(jnp.float32)

        @pl.loop(0, raw.shape[1] // LANES)
        def _(chunk):
            cols = pl.ds(pl.multiple_of(chunk * LANES, LANES), LANES)
            taps = weight[:, cols]
            shift = bias[:, cols]
            for start in range(0, rows, piece):
                base = HALO + start
                total = shift + taps[KCONV - 1 : KCONV] * wide[base : base + piece, cols]
                for tap in range(KCONV - 1):
                    low = base - (KCONV - 1) + tap
                    total = total + (
                        taps[tap : tap + 1]
                        * wide[low : low + piece, cols]
                        * match[tap, start : start + piece, :]
                    )
                out[start : start + piece, cols] = (total / (1.0 + jnp.exp(-total))).astype(
                    jnp.bfloat16
                )

    conv(raw_x, w_x, bias_x, x_out)
    conv(raw_b, w_b, bias_b, b_out)
    conv(raw_c, w_c, bias_c, c_out)
    gains = []
    for start in range(0, rows, SPAN):
        part = slice(start, start + SPAN)
        factor = dot32(tail[0, part, :], expand[...])
        weighted = (x_out[part, :].astype(jnp.float32) * factor).astype(jnp.bfloat16)
        gains.append(dot32(b_out[part, :], weighted, ((0,), (0,))))
    first_state[0] = gains[0]
    last_state[0] = (gains[0] * pass_last[0] + gains[1]).astype(jnp.bfloat16)


def mix_kernel(x_ref, b_ref, c_ref, decay_col, decay_row, step_row, seg_col, seg_row, out, scores):
    rows = x_ref.shape[0]
    lanes = lax.broadcasted_iota(jnp.int32, (SPAN, LANES), 1)
    for start in range(0, rows, SPAN):
        part = slice(start, start + SPAN)
        at_row = lax.broadcasted_iota(jnp.int32, (SPAN, SPAN), 0)
        at_col = lax.broadcasted_iota(jnp.int32, (SPAN, SPAN), 1)
        allowed = (seg_col[part, :] == seg_row[:, part]) & (at_row >= at_col)
        products = dot32(c_ref[part, :], b_ref[part, :], ((1,), (1,)))
        scores[...] = jnp.where(allowed, products, 0.0)
        for pair in range(PER_GROUP // 2):
            cols = slice(pair * LANES, (pair + 1) * LANES)
            values = x_ref[part, cols]
            halves = []
            for head in (2 * pair, 2 * pair + 1):
                spread = decay_col[0, part, head : head + 1] - decay_row[0, head : head + 1, part]
                mixing = (
                    scores[...] * jnp.exp(jnp.minimum(spread, 0.0)) * step_row[0, head : head + 1, part]
                ).astype(jnp.bfloat16)
                halves.append(dot32(mixing, values))
            out[part, cols] = jnp.where(lanes < HEAD_DIM, halves[0], halves[1])


def norm_kernel(inside, x_ref, c_ref, upper, lower, factor, expand, skip, gain, out, mixed):
    power = jnp.zeros((out.shape[0], 1), jnp.float32)
    for group in range(GROUPS):
        cols = slice(group * WIDE, (group + 1) * WIDE)
        c_mat = c_ref[:, group * STATE : (group + 1) * STATE]
        readout = dot32(c_mat, upper[0, group]) + dot32(c_mat, lower[0, group])
        total = inside[:, cols] + readout * dot32(factor[group], expand[...])
        total = total + x_ref[:, cols].astype(jnp.float32) * skip[:, cols]
        mixed[:, cols] = total
        power = power + jnp.sum(total * total, axis=1, keepdims=True)
    scale = lax.rsqrt(power / INNER + 1e-05)
    for group in range(GROUPS):
        cols = slice(group * WIDE, (group + 1) * WIDE)
        out[:, cols] = (mixed[:, cols] * scale * gain[:, cols]).astype(jnp.bfloat16)


def by_group(values):
    return values.reshape(values.shape[0], GROUPS, PER_GROUP).transpose(1, 0, 2)


def split_pair(values):
    grouped = by_group(values)
    upper = grouped.astype(jnp.bfloat16)
    lower = (grouped - upper.astype(jnp.float32)).astype(jnp.bfloat16)
    return jnp.concatenate([upper, lower], axis=2)


def along_lanes(values):
    return jnp.repeat(values, HEAD_DIM, axis=-1).reshape(values.shape[:-1] + (GROUPS, 1, WIDE))


def per_device(
    stream_tokens,
    xbc_weight,
    step_weight,
    conv_weight,
    conv_bias,
    step_bias,
    decay_rate,
    skip_gain,
    norm_gain,
    segment_ids,
    page_target,
):
    req_count = lax.axis_size("req")
    seq_count = lax.axis_size("seq")
    tok_rows = stream_tokens.shape[0]
    page_rows = tok_rows // req_count
    blocks = tok_rows // SPAN
    targets = page_target[0]
    spots = jnp.arange(req_count, dtype=jnp.int32)
    page_order = jnp.sum(jnp.where(targets[None, :] == spots[:, None], spots[None, :], 0), axis=1)
    params = pltpu.CompilerParams(vmem_limit_bytes=VMEM_LIMIT)

    pages = stream_tokens.reshape(req_count, page_rows, stream_tokens.shape[1])
    outgoing = jnp.take(pages, page_order, axis=0, mode="clip")
    tokens = lax.all_to_all(outgoing, "req", split_axis=0, concat_axis=0, tiled=True)
    tokens = tokens.reshape(tok_rows, stream_tokens.shape[1])
    prev_tokens = shifted(tokens[tok_rows - HALO :], "seq", 1)
    full_weight = lax.all_gather(xbc_weight, ("seq", "req"), axis=1, tiled=True)
    all_rows = jnp.concatenate([prev_tokens, tokens], axis=0)
    raw_all = jnp.dot(all_rows, full_weight, preferred_element_type=jnp.float32).astype(
        jnp.bfloat16
    )
    step_raw = jnp.dot(tokens, step_weight, preferred_element_type=jnp.float32).astype(jnp.bfloat16)

    seq_at = lax.axis_index("seq")
    full_ids = segment_ids[0]
    padded_ids = jnp.concatenate([jnp.full((KCONV - 1,), -1, jnp.int32), full_ids])
    labels = lax.dynamic_slice_in_dim(padded_ids, seq_at * tok_rows, tok_rows + KCONV - 1)
    seg_rows = labels[KCONV - 1 :]
    match = jnp.stack([labels[tap : tap + tok_rows] == seg_rows for tap in range(KCONV - 1)])
    match = jnp.broadcast_to(match.astype(jnp.float32)[:, :, None], (KCONV - 1, tok_rows, LANES))
    ends = seg_rows.reshape(blocks, SPAN)[:, SPAN - 1]
    before = jnp.concatenate([labels[KCONV - 2 : KCONV - 1], ends[:-1]])

    step_size = jax.nn.softplus(step_raw.astype(jnp.float32) + step_bias[None, :])
    log_decay = jnp.cumsum(
        (-step_size * decay_rate[None, :]).reshape(blocks, SPAN, HEADS), axis=1
    )
    last_decay = log_decay[:, SPAN - 1]
    seg_blocks = seg_rows.reshape(blocks, SPAN)
    keep = (seg_blocks == before[:, None])[:, :, None]
    factor = split_pair(jnp.where(keep, jnp.exp(log_decay), 0.0).reshape(tok_rows, HEADS))
    in_tail = (seg_blocks == ends[:, None])[:, :, None]
    tail = jnp.where(in_tail, jnp.exp(last_decay[:, None] - log_decay), 0.0).reshape(tok_rows, HEADS)
    tail = split_pair(tail * step_size)
    passing = jnp.where((ends == before)[:, None], jnp.exp(last_decay), 0.0)
    all_through = lax.all_gather(passing[0] * passing[1], "seq")
    running = jnp.ones((HEADS,), jnp.float32)
    shares = [None] * seq_count
    for turn in range(seq_count - 1, -1, -1):
        shares[turn] = jnp.where(turn < seq_at, running, 0.0)
        running = jnp.where(turn < seq_at, running * all_through[turn], running)
    shares = along_lanes(jnp.stack(shares))
    passing = along_lanes(passing)
    flat_decay = log_decay.reshape(tok_rows, HEADS)
    decay_col = by_group(flat_decay)
    decay_row = flat_decay.T.reshape(GROUPS, PER_GROUP, tok_rows)
    step_row = step_size.T.reshape(GROUPS, PER_GROUP, tok_rows)
    owner = jnp.arange(WIDE) // HEAD_DIM
    expand = (owner[None, :] == (jnp.arange(2 * PER_GROUP) % PER_GROUP)[:, None]).astype(
        jnp.bfloat16
    )

    bias_row = conv_bias[None, :]
    at_b = INNER // STATE
    at_c = at_b + GROUPS
    raw_len = tok_rows + HALO

    def columns(height, width, at):
        return pl.BlockSpec((height, width), lambda group: (0, at + group))

    def of_group(*shape):
        return pl.BlockSpec((1,) + shape, lambda group: (group, 0, 0))

    def whole(*shape):
        return pl.BlockSpec(shape, lambda step: (0,) * len(shape))

    x_all, b_all, c_all, first_state, last_state = pl.pallas_call(
        conv_kernel,
        grid=(GROUPS,),
        in_specs=[
            columns(raw_len, WIDE, 0),
            columns(raw_len, STATE, at_b),
            columns(raw_len, STATE, at_c),
            columns(KCONV, WIDE, 0),
            columns(KCONV, STATE, at_b),
            columns(KCONV, STATE, at_c),
            columns(1, WIDE, 0),
            columns(1, STATE, at_b),
            columns(1, STATE, at_c),
            whole(KCONV - 1, tok_rows, LANES),
            of_group(tok_rows, 2 * PER_GROUP),
            of_group(1, WIDE),
            whole(2 * PER_GROUP, WIDE),
        ],
        out_specs=[
            columns(tok_rows, WIDE, 0),
            columns(tok_rows, STATE, 0),
            columns(tok_rows, STATE, 0),
            of_group(STATE, WIDE),
            of_group(STATE, WIDE),
        ],
        out_shape=[
            jax.ShapeDtypeStruct((tok_rows, INNER), jnp.bfloat16),
            jax.ShapeDtypeStruct((tok_rows, GROUPS * STATE), jnp.bfloat16),
            jax.ShapeDtypeStruct((tok_rows, GROUPS * STATE), jnp.bfloat16),
            jax.ShapeDtypeStruct((GROUPS, STATE, WIDE), jnp.float32),
            jax.ShapeDtypeStruct((GROUPS, STATE, WIDE), jnp.bfloat16),
        ],
        scratch_shapes=[pltpu.VMEM((raw_len, WIDE), jnp.float32)],
        compiler_params=params,
        cost_estimate=pl.CostEstimate(
            flops=2 * tok_rows * INNER * STATE, bytes_accessed=14 << 20, transcendentals=tok_rows * XBC
        ),
    )(
        raw_all, raw_all, raw_all, conv_weight, conv_weight, conv_weight,
        bias_row, bias_row, bias_row, match, tail, passing[1], expand,
    )
    all_states = lax.all_gather(last_state, "seq")

    inside = pl.pallas_call(
        mix_kernel,
        grid=(GROUPS,),
        in_specs=[
            columns(tok_rows, WIDE, 0),
            columns(tok_rows, STATE, 0),
            columns(tok_rows, STATE, 0),
            of_group(tok_rows, PER_GROUP),
            of_group(PER_GROUP, tok_rows),
            of_group(PER_GROUP, tok_rows),
            whole(tok_rows, 1),
            whole(1, tok_rows),
        ],
        out_specs=columns(tok_rows, WIDE, 0),
        out_shape=jax.ShapeDtypeStruct((tok_rows, INNER), jnp.float32),
        scratch_shapes=[pltpu.VMEM((SPAN, SPAN), jnp.float32)],
        compiler_params=params,
        cost_estimate=pl.CostEstimate(
            flops=16 * tok_rows * SPAN * INNER,
            bytes_accessed=14 << 20,
            transcendentals=tok_rows * SPAN * HEADS,
        ),
    )(x_all, b_all, c_all, decay_col, decay_row, step_row, seg_rows[:, None], seg_rows[None, :])

    incoming = jnp.sum(shares * all_states.astype(jnp.float32), axis=0)
    states = jnp.stack([incoming, passing[0] * incoming + first_state])
    upper = states.astype(jnp.bfloat16)
    lower = (states - upper.astype(jnp.float32)).astype(jnp.bfloat16)

    tile = SPAN // 2
    per_block = SPAN // tile
    normed = pl.pallas_call(
        norm_kernel,
        grid=(tok_rows // tile,),
        in_specs=[
            pl.BlockSpec((tile, INNER), lambda step: (step, 0)),
            pl.BlockSpec((tile, INNER), lambda step: (step, 0)),
            pl.BlockSpec((tile, GROUPS * STATE), lambda step: (step, 0)),
            pl.BlockSpec((1, GROUPS, STATE, WIDE), lambda step: (step // per_block, 0, 0, 0)),
            pl.BlockSpec((1, GROUPS, STATE, WIDE), lambda step: (step // per_block, 0, 0, 0)),
            pl.BlockSpec((GROUPS, tile, 2 * PER_GROUP), lambda step: (0, step, 0)),
            whole(2 * PER_GROUP, WIDE),
            whole(1, INNER),
            whole(1, INNER),
        ],
        out_specs=pl.BlockSpec((tile, INNER), lambda step: (step, 0)),
        out_shape=jax.ShapeDtypeStruct((tok_rows, INNER), jnp.bfloat16),
        scratch_shapes=[pltpu.VMEM((tile, INNER), jnp.float32)],
        compiler_params=params,
        cost_estimate=pl.CostEstimate(
            flops=4 * tok_rows * INNER * STATE, bytes_accessed=22 << 20, transcendentals=tok_rows
        ),
    )(
        inside, x_all, c_all, upper, lower, factor, expand,
        jnp.repeat(skip_gain, HEAD_DIM)[None, :], norm_gain[None, :],
    )
    returned = lax.all_to_all(
        normed.reshape(req_count, page_rows, INNER), "req", split_axis=0, concat_axis=0, tiled=True
    )
    return jnp.take(returned, targets, axis=0, mode="clip").reshape(tok_rows, INNER)


def solution(mesh):
    in_specs = (
        P(("seq", "req"), None),
        P(None, ("seq", "req")),
        P(),
        P(),
        P(),
        P(),
        P(),
        P(),
        P(),
        P("req", None),
        P(("seq", "req"), None),
    )
    out_specs = P(("seq", "req"), None)
    return jax.shard_map(
        per_device, mesh=mesh, in_specs=in_specs, out_specs=out_specs, check_vma=False
    )
```

time: 512 us -> 394 us (0.77)
  local copies, waits for them, and re-layouts: 80.4 us -> 29.4 us
  matrix products: 58 us -> 18 us
  Pallas kernels: 0 us -> 34.9 us
  other arithmetic: 47.9 us -> 14 us
  waiting for transfers between devices: 284 us -> 260 us
    dot_general x12 -> x0, matrix products: 39.4 us -> none  [the longest x2 18.6 us: span_step(): jnp.einsum('ghtu,ughp->tghp', mixing, x_heads.reshape(span_len, group_cou...]
    pallas_call x0 -> x3, Pallas kernels: none -> 34.9 us  [the longest x1 16.1 us: per_device(): pl.pallas_call(conv_kernel, grid=(GROUPS,), in_specs=[columns(raw_len, WI...]
    convert_element_type x7 -> x6, other arithmetic: 25.1 us -> 1.06 us  [the longest x1 0.58 us: per_device(): lower = (states - upper.astype(jnp.float32)).astype(jnp.bfloat16)]
    dynamic_update_slice x4 -> x0, local copies, waits for them, and re-layouts: 20.6 us -> none  [per_device(): lax.scan(partial(span_step, decay_rate), jnp.zeros((HEADS, HEAD_DIM, STAT...]
    all_gather x1, waiting for transfers between devices: 38.2 us -> 18.3 us  [per_device(): all_states = lax.all_gather(last_state, 'seq')]
    another operation x11 -> x10, local copies, waits for them, and re-layouts: 13.5 us -> 2.74 us  [the longest x3 1.55 us: by_group(): return values.reshape(values.shape[0], GROUPS, PER_GROUP).transpose(1, 0, 2)]
    reshape x4, local copies, waits for them, and re-layouts: 9.22 us -> 0.71 us  [the longest x1 0.67 us: per_device(): flat_decay = log_decay.reshape(tok_rows, HEADS)]
    slice x13 -> x6, local copies, waits for them, and re-layouts: 9.04 us -> 1.77 us  [the longest x2 1.16 us: per_device(): before = jnp.concatenate([labels[KCONV - 2:KCONV - 1], ends[:-1]])]
  transfers between devices with their start and end apart: 5 -> 5, of which waited for: 5 -> 4; matrix products, arithmetic and copies ran while one was open for 3% -> 5% of each run, Pallas kernels for 0% -> 3%
where the time goes in v2:
time: 394 us; the launch traced here: 393 us
  waiting for transfers between devices  260 us (66%)
  Pallas kernels  34.9 us (9%)
  local copies, waits for them, and re-layouts  29.4 us (7%)
  matrix products  18 us (5%)
  starting transfers between devices  14.6 us (4%)
  other arithmetic  14 us (4%)
  between operations  13.9 us (4%)
  blocking collectives  8.06 us (2%)
    all_to_all x1, waiting for transfers between devices, per_device(): lax.all_to_all(normed.reshape(req_count, page_rows, INNER), 'req', split_...  94.1 us
    all_to_all x1, waiting for transfers between devices, per_device(): lax.all_to_all(outgoing, 'req', split_axis=0, concat_axis=0, tiled=True)  83.5 us
    all_gather x1, waiting for transfers between devices, per_device(): full_weight = lax.all_gather(xbc_weight, ('seq', 'req'), axis=1, tiled=True)  63.8 us
    all_gather x1, waiting for transfers between devices, per_device(): all_states = lax.all_gather(last_state, 'seq')  18.3 us
    dot_general x1, matrix products, per_device(): jnp.dot(all_rows, full_weight, preferred_element_type=jnp.float32)  17.1 us
    pallas_call x1, Pallas kernels, per_device(): pl.pallas_call(conv_kernel, grid=(GROUPS,), in_specs=[columns(raw_len, WI...  16.1 us
    unnamed x58, local copies, waits for them, and re-layouts  12.9 us
    pallas_call x1, Pallas kernels, per_device(): pl.pallas_call(mix_kernel, grid=(GROUPS,), in_specs=[columns(tok_rows, WI...  11.4 us
  transfers between devices with their start and end apart: 5, of which 4 were waited for; matrix products, arithmetic and copies ran while one was open for 5% of the time, Pallas kernels for 3%

profile of v2, /device:TPU:0, one launch (start us, length us, event | category | flops | bytes accessed | tf_op | source)
XLA Modules:
  0.0 393.1 jit_solution(2197945310867810099)
XLA Ops:
  6.5 0.7 all-gather.5.cloned.1.call-update
  7.3 0.8 select_reduce_fusion
  8.0 0.1 copy-done
  8.1 2.0 gather_fusion
  10.1 6.5 %all-to-all-start = ((bf16[8,64,2048]{2,1,0:T(8,128)(2,1)}), bf16[8,64,2048]{2,1,0:T(8,128)(2,1)S(1)}, u32[]{:S(2)}, u32[]{:S(2)}) async-start(bf16[8,64,2048]{2,1,0:T(8,128)(2,1)} %gather_fusion), calls=%async_computation | async-start | bytes 4194304 | tf_op jit(solution)/shard_map/all_to_all | solution.py:158
  16.7 0.1 pad_dynamic-slice_fusion
  16.8 0.5 slice.70
  17.5 0.6 slice.90
  18.1 1.2 pad_add_fusion
  19.4 0.2 slice_reduce_fusion.2
  19.5 1.4 compare_reduce_fusion
  21.0 0.1 compare_convert_fusion.expand
  21.1 83.5 %all-to-all-done = bf16[8,64,2048]{2,1,0:T(8,128)(2,1)S(1)} async-done(((bf16[8,64,2048]{2,1,0:T(8,128)(2,1)}), bf16[8,64,2048]{2,1,0:T(8,128)(2,1)S(1)}, u32[]{:S(2)}, u32[]{:S(2)}) %all-to-all-start) | async-done | bytes 2097184 | tf_op jit(solution)/shard_map/all_to_all | solution.py:158
  104.6 3.3 collective-permute-start
  108.0 0.8 negate_multiply_fusion
  108.8 1.2 reduce-window.6
  110.0 0.2 slice_reduce_fusion
  110.3 0.8 bitcast_bitcast_fusion
  111.0 0.2 slice_reduce_fusion.1
  111.2 0.8 exponential_select_fusion
  112.0 0.1 fusion.12
  112.1 0.3 copy.50.tail
  112.5 1.1 slice_reduce_fusion.3
  113.5 0.1 broadcast_in_dim.119
  113.7 0.1 broadcast_in_dim.121.pass_last
  113.8 63.8 %all-gather.5.cloned.1.call-done = bf16[2048,5120]{0,1:T(8,128)(2,1)} async-done(((bf16[2048,160]{0,1:T(8,128)(2,1)}), bf16[2048,5120]{0,1:T(8,128)(2,1)}) %all-gather.5.cloned.1.call-update) | async-done | bytes 20971536 | tf_op jit(solution)/shard_map/all_gather | solution.py:161
  177.7 17.1 %convolution_convert_fusion.raw_x.raw_b.raw_c = bf16[528,5120]{1,0:T(8,128)(2,1)} fusion(bf16[2048,5120]{0,1:T(8,128)(2,1)} %all-gather.5.cloned.1.call-done, bf16[512,2048]{1,0:T(8,128)(2,1)S(1)} %bitcast.122, bf16[16,2048]{1,0:T(8,128)(2,1)S(1)} %collective-permute-done), kind=kOutput, calls=%fused_computation.4 | convolution fusion | flops 11079991296 | bytes 28540928 | tf_op jit(solution)/shard_map/dot_general | solution.py:163
  194.8 0.3 broadcast_in_dim.113.match
  195.1 16.1 %shard_map.109 = (bf16[512,4096]{1,0:T(8,128)(2,1)S(1)}, bf16[512,512]{1,0:T(8,128)(2,1)S(1)}, bf16[512,512]{1,0:T(8,128)(2,1)S(1)}, f32[4,128,1024]{2,1,0:T(8,128)S(1)}, bf16[4,128,1024]{2,1,0:T(8,128)(2,1)S(1)}) custom-call(bf16[528,5120]{1,0:T(8,128)(2,1)} %convolution_convert_fusion.raw_x.raw_b.raw_c, ...), custom_call_target="tpu_custom_call" | custom-call | flops 536870912 | bytes 14680064 | tf_op jit(solution)/shard_map/pallas_call | solution.py:221
  211.2 2.0 copy-done.3
  213.3 1.0 copy-done.9
  214.3 0.8 copy-done.16
  215.1 1.2 copy.54.seg_col
  216.3 0.7 broadcast_in_dim.131
  217.0 0.1 broadcast_in_dim_reshape.3.skip
  217.2 1.0 copy.51
  218.2 0.1 reshape_reshape.8
  218.3 1.3 copy.52
  219.7 0.7 copy.61
  220.3 8.1 %all-gather.1 = f32[4,1,64]{2,1,0:T(1,128)S(1)} all-gather(f32[1,1,64]{2,1,0:T(1,128)S(1)} %copy-done.25), channel_id=1, replica_groups=mesh['seq'=4,'req'=8] {'seq'}, dimensions={0}, use_global_device_ids=true | all-gather | bytes 1280 | tf_op jit(solution)/shard_map/all_gather | solution.py:190
  228.5 0.1 broadcast_in_dim.126
  228.6 0.8 mul.52
  229.4 0.1 broadcast_in_dim.127
  229.5 0.1 broadcast_in_dim.129
  229.6 0.1 copy.55
  229.7 0.1 reshape_reshape.9
  229.9 0.3 copy.56.factor
  230.2 1.0 compare_select_fusion
  231.2 2.2 copy-done.4
  233.4 1.2 copy-done.8
  234.6 0.9 copy-done.12
  235.5 1.0 copy-done.17
  236.5 11.4 %shard_map.110.inside = f32[512,4096]{1,0:T(8,128)} custom-call(bf16[512,4096]{1,0:T(8,128)(2,1)S(1)} %copy-done.4, bf16[512,512]{1,0:T(8,128)(2,1)S(1)} %copy-done.17, bf16[512,512]{1,0:T(8,128)(2,1)S(1)} %get-tuple-element.12.c_ref, f32[4,512,16]{2,1,0:T(8,128)S(1)} %bitcast.109, f32[4,16,512]{2,1,0:T(8,128)S(1)} %bitcast.113, ...), custom_call_target="tpu_custom_call" | custom-call | flops 8589934592 | bytes 14680064 | tf_op jit(solution)/shard_map/pallas_call | solution.py:264
  247.9 18.3 %all-gather.7.cloned.1.call-done = bf16[16,128,1024]{2,1,0:T(8,128)(2,1)} async-done(((bf16[4,128,1024]{2,1,0:T(8,128)(2,1)}), bf16[16,128,1024]{2,1,0:T(8,128)(2,1)}) %all-gather.7.cloned.1.call-update) | async-done | bytes 4194320 | tf_op jit(solution)/shard_map/all_gather | solution.py:262
  266.2 3.6 fusion
  269.8 0.6 add_bitcast_fusion
  270.4 0.4 fusion.1.upper
  270.8 0.6 subtract_convert_fusion.lower
  271.4 1.6 copy-done.5
  273.0 7.4 %shard_map.111 = bf16[512,4096]{1,0:T(8,128)(2,1)S(1)} custom-call(f32[512,4096]{1,0:T(8,128)} %shard_map.110.inside, bf16[512,4096]{1,0:T(8,128)(2,1)S(1)} %copy-done.5, bf16[512,512]{1,0:T(8,128)(2,1)S(1)} %get-tuple-element.12.c_ref, bf16[2,4,128,1024]{3,2,1,0:T(8,128)(2,1)S(1)} %fusion.1.upper, bf16[2,4,128,1024]{3,2,1,0:T(8,128)(2,1)S(1)} %subtract_convert_fusion.lower, ...), custom_call_target="tpu_custom_call" | custom-call | flops 1073741824 | bytes 23068672 | tf_op jit(solution)/shard_map/pallas_call | solution.py:295
  280.4 2.0 copy-done.2
  282.4 4.7 %all-to-all-start.1 = ((bf16[8,64,4096]{2,1,0:T(8,128)(2,1)}), bf16[8,64,4096]{2,1,0:T(8,128)(2,1)}, u32[]{:S(2)}, u32[]{:S(2)}) async-start(bf16[8,64,4096]{2,1,0:T(8,128)(2,1)} %bitcast.108), calls=%async_computation.1 | async-start | bytes 8388608 | tf_op jit(solution)/shard_map/all_to_all | solution.py:320
  287.1 94.1 %all-to-all-done.1 = bf16[8,64,4096]{2,1,0:T(8,128)(2,1)} async-done(((bf16[8,64,4096]{2,1,0:T(8,128)(2,1)}), bf16[8,64,4096]{2,1,0:T(8,128)(2,1)}, u32[]{:S(2)}, u32[]{:S(2)}) %all-to-all-start.1) | async-done | bytes 4194336 | tf_op jit(solution)/shard_map/all_to_all | solution.py:320
  381.2 5.0 %gather_fusion.1 = bf16[8,64,4096]{2,1,0:T(8,128)(2,1)} fusion(bf16[8,64,4096]{2,1,0:T(8,128)(2,1)} %all-to-all-done.1, s32[1024]{0:T(1024)S(1)} %pad_clamp_fusion), kind=kCustom, calls=%fused_computation.1 | custom fusion | bytes 8388640 | tf_op jit(solution)/shard_map/jit(_take)/gather | solution.py:323
  (80 shorter events, 1.0 us)
Async XLA Ops:
  6.5 1.6 copy-start
  6.5 171.1 %all-gather.5.cloned.1.call-start = ((), (), s32[]{:S(2)}) async-start(), calls=%async_computation.2 | async-start | bytes 21626880 | tf_op jit(solution)/shard_map/all_gather | solution.py:161
  10.1 6.5 %copy-start.23 = (s32[1,2048]{1,0:T(1,128)S(1)}, s32[1,2048]{1,0:T(1,128)}, u32[]{:S(2)}) copy-start(s32[1,2048]{1,0:T(1,128)} %param.20) | copy-start | bytes 24580
  10.1 97.8 %copy-start.22 = (bf16[2048,64]{0,1:T(8,128)(2,1)S(1)}, bf16[2048,64]{0,1:T(8,128)(2,1)}, u32[]{:S(2)}) copy-start(bf16[2048,64]{0,1:T(8,128)(2,1)} %param.13) | copy-start | bytes 786436
  10.1 97.8 %copy-start.26 = (f32[64]{0:T(128)S(1)}, f32[64]{0:T(128)}, u32[]{:S(2)}) copy-start(f32[64]{0:T(128)} %param.17) | copy-start | bytes 772
  10.1 97.8 %copy-start.27 = (f32[64]{0:T(128)S(1)}, f32[64]{0:T(128)}, u32[]{:S(2)}) copy-start(f32[64]{0:T(128)} %param.16) | copy-start | bytes 772
  10.1 94.4 %all-to-all-start = ((bf16[8,64,2048]{2,1,0:T(8,128)(2,1)}), bf16[8,64,2048]{2,1,0:T(8,128)(2,1)S(1)}, u32[]{:S(2)}, u32[]{:S(2)}) async-start(bf16[8,64,2048]{2,1,0:T(8,128)(2,1)} %gather_fusion), calls=%async_computation | async-start | bytes 4194304 | tf_op jit(solution)/shard_map/all_to_all | solution.py:158
  16.6 249.5 %all-gather.7.cloned.1.call-start = ((), (), s32[]{:S(2)}) async-start(), calls=%async_computation.3 | async-start | bytes 5242880 | tf_op jit(solution)/shard_map/all_gather | solution.py:262
  16.8 178.0 %copy-start.13 = (s32[512]{0:T(512)}, s32[512]{0:T(512)S(1)}, u32[]{:S(2)}) copy-start(s32[512]{0:T(512)S(1)} %slice.62) | copy-start | bytes 6148
  104.6 9.2 %collective-permute-start = (bf16[16,2048]{1,0:T(8,128)(2,1)S(1)}, bf16[16,2048]{1,0:T(8,128)(2,1)S(1)}, u32[]{:S(2)}, u32[]{:S(2)}) collective-permute-start(bf16[16,2048]{1,0:T(8,128)(2,1)S(1)} %slice.85), channel_id=1, source_target_pairs={{0,8},{8,16},{16,24},{1,9},{9,17},{17,25},{2,10},{10,18},{18,26},{... | collective-permute-start | bytes 196616 | tf_op jit(solution)/shard_map/ppermute | solution.py:23
  108.8 86.0 %copy-start.18 = (f32[512,64]{0,1:T(8,128)}, f32[512,64]{0,1:T(8,128)S(1)}, u32[]{:S(2)}) copy-start(f32[512,64]{0,1:T(8,128)S(1)} %get-tuple-element.35) | copy-start | bytes 393220
  111.0 83.8 %copy-start.19 = (f32[2,256,64]{1,2,0:T(8,128)}, f32[2,256,64]{1,2,0:T(8,128)S(1)}, u32[]{:S(2)}) copy-start(f32[2,256,64]{1,2,0:T(8,128)S(1)} %get-tuple-element.26) | copy-start | bytes 393220
  113.8 81.3 %copy-start.10 = (f32[4,5120]{1,0:T(4,128)S(1)}, f32[4,5120]{1,0:T(4,128)}, u32[]{:S(2)}) copy-start(f32[4,5120]{1,0:T(4,128)} %w_c.1) | copy-start | bytes 245764
  113.8 81.3 %copy-start.11 = (f32[5120]{0:T(1024)S(1)}, f32[5120]{0:T(1024)}, u32[]{:S(2)}) copy-start(f32[5120]{0:T(1024)} %param.15) | copy-start | bytes 61444
  211.2 2.0 copy-start.3
  213.3 1.0 copy-start.9
  214.3 0.8 copy-start.16
  215.1 14.8 %copy-start.6 = (f32[4,128,1024]{2,1,0:T(8,128)}, f32[4,128,1024]{2,1,0:T(8,128)S(1)}, u32[]{:S(2)}) copy-start(f32[4,128,1024]{2,1,0:T(8,128)S(1)} %get-tuple-element.14) | copy-start | bytes 6291460
  215.1 4.6 %copy-start.21 = (f32[2,8,8,256]{3,2,1,0:T(8,128)S(1)}, f32[2,8,8,256]{3,2,1,0:T(8,128)}, u32[]{:S(2)}) copy-start(f32[2,8,8,256]{3,2,1,0:T(8,128)} %get-tuple-element.25) | copy-start | bytes 393220
  215.1 5.3 %copy-start.25 = (f32[1,1,64]{2,1,0:T(1,128)S(1)}, f32[1,1,64]{2,1,0:T(1,128)}, u32[]{:S(2)}) copy-start(f32[1,1,64]{2,1,0:T(1,128)} %get-tuple-element.33) | copy-start | bytes 772
  215.1 14.3 %copy-start.24 = (f32[64]{0:T(128)S(1)}, f32[64]{0:T(128)}, u32[]{:S(2)}) copy-start(f32[64]{0:T(128)} %get-tuple-element.15) | copy-start | bytes 772
  215.1 14.5 %copy-start.20 = (f32[2,256,64]{1,2,0:T(8,128)S(1)}, f32[2,256,64]{1,2,0:T(8,128)}, u32[]{:S(2)}) copy-start(f32[2,256,64]{1,2,0:T(8,128)} %get-tuple-element.23) | copy-start | bytes 393220
  217.2 13.9 %copy-start.14 = (s32[512]{0:T(512)S(1)}, s32[512]{0:T(512)}, u32[]{:S(2)}) copy-start(s32[512]{0:T(512)} %copy-done.13) | copy-start | bytes 6148
  231.2 2.2 copy-start.4
  233.4 1.2 copy-start.8
  234.6 0.9 copy-start.12
  235.5 1.0 copy-start.17
  266.1 3.6 copy-start.7
  270.8 2.2 copy-start.5
  270.8 2.2 copy-start.15
  280.4 2.0 copy-start.2
  282.4 4.7 %copy-start.28 = (s32[1,8]{1,0:T(1,128)S(1)}, s32[1,8]{1,0:T(1,128)}, u32[]{:S(2)}) copy-start(s32[1,8]{1,0:T(1,128)} %param.21) | copy-start | bytes 100
  282.4 98.8 %all-to-all-start.1 = ((bf16[8,64,4096]{2,1,0:T(8,128)(2,1)}), bf16[8,64,4096]{2,1,0:T(8,128)(2,1)}, u32[]{:S(2)}, u32[]{:S(2)}) async-start(bf16[8,64,4096]{2,1,0:T(8,128)(2,1)} %bitcast.108), calls=%async_computation.1 | async-start | bytes 8388608 | tf_op jit(solution)/shard_map/all_to_all | solution.py:320
  287.1 99.1 %copy-start.1 = (bf16[512,2048]{1,0:T(8,128)(2,1)S(1)}, bf16[512,2048]{1,0:T(8,128)(2,1)}, u32[]{:S(2)}) copy-start(bf16[512,2048]{1,0:T(8,128)(2,1)} %param.11) | copy-start | bytes 6291460
Sparse Core Ops, SparseCore 0:
  10.2 167.4 all-gather.4
  215.2 50.8 all-gather.6

commit v3 on v2

--- a/solution.py
+++ b/solution.py
@@ -35,7 +35,7 @@
 
 
 def conv_kernel(
-    raw_x, raw_b, raw_c, w_x, w_b, w_c, bias_x, bias_b, bias_c, match, tail, pass_last, expand,
+    raw_x, raw_b, raw_c, w_x, w_b, w_c, bias_x, bias_b, bias_c, match, tail, pass_last, through, expand,
     x_out, b_out, c_out, first_state, last_state, wide,
 ):
     rows = x_out.shape[0]
@@ -73,7 +73,15 @@
         weighted = (x_out[part, :].astype(jnp.float32) * factor).astype(jnp.bfloat16)
         gains.append(dot32(b_out[part, :], weighted, ((0,), (0,))))
     first_state[0] = gains[0]
-    last_state[0] = (gains[0] * pass_last[0] + gains[1]).astype(jnp.bfloat16)
+    last_state[0, :STATE] = (gains[0] * pass_last[0] + gains[1]).astype(jnp.bfloat16)
+    rest = jnp.broadcast_to(through[0], (HALO, WIDE))
+    row = lax.broadcasted_iota(jnp.int32, (HALO, WIDE), 0)
+    extra = jnp.zeros((HALO, WIDE), jnp.float32)
+    for place in range(3):
+        part = rest.astype(jnp.bfloat16).astype(jnp.float32)
+        extra = jnp.where(row == place, part, extra)
+        rest = rest - part
+    last_state[0, STATE:] = extra.astype(jnp.bfloat16)
 
 
 def mix_kernel(x_ref, b_ref, c_ref, decay_col, decay_row, step_row, seg_col, seg_row, out, scores):
@@ -158,11 +166,27 @@
     tokens = lax.all_to_all(outgoing, "req", split_axis=0, concat_axis=0, tiled=True)
     tokens = tokens.reshape(tok_rows, stream_tokens.shape[1])
     prev_tokens = shifted(tokens[tok_rows - HALO :], "seq", 1)
-    full_weight = lax.all_gather(xbc_weight, ("seq", "req"), axis=1, tiled=True)
     all_rows = jnp.concatenate([prev_tokens, tokens], axis=0)
-    raw_all = jnp.dot(all_rows, full_weight, preferred_element_type=jnp.float32).astype(
-        jnp.bfloat16
-    )
+    depth = xbc_weight.shape[0] // 2
+    core = lax.rem(lax.axis_index("req"), 2)
+    swap = [(i, i ^ 1) for i in range(req_count)]
+    mine = lax.dynamic_slice_in_dim(xbc_weight, core * depth, depth, axis=0)
+    given = lax.dynamic_slice_in_dim(xbc_weight, (1 - core) * depth, depth, axis=0)
+    taken = lax.ppermute(given, "req", swap)
+    chip_half = jnp.concatenate(
+        [jnp.where(core == 0, mine, taken), jnp.where(core == 0, taken, mine)], axis=1
+    )
+    device_count = seq_count * req_count
+    same_core = [list(range(first, device_count, 2)) for first in range(2)]
+    near_half = lax.all_gather(
+        chip_half, ("seq", "req"), axis=1, tiled=True, axis_index_groups=same_core
+    )
+    far_half = lax.ppermute(near_half, "req", swap)
+    near_rows = lax.dynamic_slice_in_dim(all_rows, core * depth, depth, axis=1)
+    far_rows = lax.dynamic_slice_in_dim(all_rows, (1 - core) * depth, depth, axis=1)
+    raw_near = jnp.dot(near_rows, near_half, preferred_element_type=jnp.float32)
+    raw_far = jnp.dot(far_rows, far_half, preferred_element_type=jnp.float32)
+    raw_all = (raw_near + raw_far).astype(jnp.bfloat16)
     step_raw = jnp.dot(tokens, step_weight, preferred_element_type=jnp.float32).astype(jnp.bfloat16)
 
     seq_at = lax.axis_index("seq")
@@ -187,13 +211,7 @@
     tail = jnp.where(in_tail, jnp.exp(last_decay[:, None] - log_decay), 0.0).reshape(tok_rows, HEADS)
     tail = split_pair(tail * step_size)
     passing = jnp.where((ends == before)[:, None], jnp.exp(last_decay), 0.0)
-    all_through = lax.all_gather(passing[0] * passing[1], "seq")
-    running = jnp.ones((HEADS,), jnp.float32)
-    shares = [None] * seq_count
-    for turn in range(seq_count - 1, -1, -1):
-        shares[turn] = jnp.where(turn < seq_at, running, 0.0)
-        running = jnp.where(turn < seq_at, running * all_through[turn], running)
-    shares = along_lanes(jnp.stack(shares))
+    through = along_lanes(passing[0] * passing[1])
     passing = along_lanes(passing)
     flat_decay = log_decay.reshape(tok_rows, HEADS)
     decay_col = by_group(flat_decay)
@@ -234,6 +252,7 @@
             whole(KCONV - 1, tok_rows, LANES),
             of_group(tok_rows, 2 * PER_GROUP),
             of_group(1, WIDE),
+            of_group(1, WIDE),
             whole(2 * PER_GROUP, WIDE),
         ],
         out_specs=[
@@ -241,14 +260,14 @@
             columns(tok_rows, STATE, 0),
             columns(tok_rows, STATE, 0),
             of_group(STATE, WIDE),
-            of_group(STATE, WIDE),
+            of_group(STATE + HALO, WIDE),
         ],
         out_shape=[
             jax.ShapeDtypeStruct((tok_rows, INNER), jnp.bfloat16),
             jax.ShapeDtypeStruct((tok_rows, GROUPS * STATE), jnp.bfloat16),
             jax.ShapeDtypeStruct((tok_rows, GROUPS * STATE), jnp.bfloat16),
             jax.ShapeDtypeStruct((GROUPS, STATE, WIDE), jnp.float32),
-            jax.ShapeDtypeStruct((GROUPS, STATE, WIDE), jnp.bfloat16),
+            jax.ShapeDtypeStruct((GROUPS, STATE + HALO, WIDE), jnp.bfloat16),
         ],
         scratch_shapes=[pltpu.VMEM((raw_len, WIDE), jnp.float32)],
         compiler_params=params,
@@ -257,7 +276,7 @@
         ),
     )(
         raw_all, raw_all, raw_all, conv_weight, conv_weight, conv_weight,
-        bias_row, bias_row, bias_row, match, tail, passing[1], expand,
+        bias_row, bias_row, bias_row, match, tail, passing[1], through, expand,
     )
     all_states = lax.all_gather(last_state, "seq")
 
@@ -285,7 +304,13 @@
         ),
     )(x_all, b_all, c_all, decay_col, decay_row, step_row, seg_rows[:, None], seg_rows[None, :])
 
-    incoming = jnp.sum(shares * all_states.astype(jnp.float32), axis=0)
+    all_through = jnp.sum(all_states[:, :, STATE : STATE + 3].astype(jnp.float32), axis=2, keepdims=True)
+    running = jnp.ones((GROUPS, 1, WIDE), jnp.float32)
+    incoming = jnp.zeros((GROUPS, STATE, WIDE), jnp.float32)
+    for turn in range(seq_count - 2, -1, -1):
+        share = jnp.where(turn < seq_at, running, 0.0)
+        incoming = incoming + share * all_states[turn, :, :STATE].astype(jnp.float32)
+        running = jnp.where(turn < seq_at, running * all_through[turn], running)
     states = jnp.stack([incoming, passing[0] * incoming + first_state])
     upper = states.astype(jnp.bfloat16)
     lower = (states - upper.astype(jnp.float32)).astype(jnp.bfloat16)

time: 394 us -> 441 us (1.12)
  waiting for transfers between devices: 260 us -> 308 us
  matrix products: 18 us -> 26.5 us
  blocking collectives: 8.06 us -> 0 us
    all_gather x1, waiting for transfers between devices: 63.8 us -> 135 us  [per_device(): lax.all_gather(chip_half, ('seq', 'req'), axis=1, tiled=True, axis_index_...]
    all_to_all x1, waiting for transfers between devices: 83.5 us -> 44.5 us  [per_device(): lax.all_to_all(outgoing, 'req', split_axis=0, concat_axis=0, tiled=True)]
    all_gather x1, waiting for transfers between devices: 18.3 us -> 32.7 us  [per_device(): all_states = lax.all_gather(last_state, 'seq')]
    dot_general x1 -> x2, matrix products: 17.1 us -> 25.7 us  [the longest x1 13.2 us: per_device(): raw_near = jnp.dot(near_rows, near_half, preferred_element_type=jnp.float32)]
    all_gather x1 -> x0, blocking collectives: 8.06 us -> none  [per_device(): all_through = lax.all_gather(passing[0] * passing[1], 'seq')]
    unnamed x58 -> x52, local copies, waits for them, and re-layouts: 12.9 us -> 13.5 us
  transfers between devices with their start and end apart: 5 -> 7, of which waited for: 4 -> 5; matrix products, arithmetic and copies ran while one was open for 5% -> 4% of each run, Pallas kernels for 3% -> 3%
where the time goes in v3:
time: 441 us
  waiting for transfers between devices  308 us (70%)
  Pallas kernels  34.9 us (8%)
  local copies, waits for them, and re-layouts  29 us (7%)
  matrix products  26.5 us (6%)
  other arithmetic  16.5 us (4%)
  between operations  13.9 us (3%)
  starting transfers between devices  12.2 us (3%)
    all_gather x1, waiting for transfers between devices, per_device(): lax.all_gather(chip_half, ('seq', 'req'), axis=1, tiled=True, axis_index_...  135 us
    all_to_all x1, waiting for transfers between devices, per_device(): lax.all_to_all(normed.reshape(req_count, page_rows, INNER), 'req', split_...  94.1 us
    all_to_all x1, waiting for transfers between devices, per_device(): lax.all_to_all(outgoing, 'req', split_axis=0, concat_axis=0, tiled=True)  44.5 us
    all_gather x1, waiting for transfers between devices, per_device(): all_states = lax.all_gather(last_state, 'seq')  32.7 us
    pallas_call x1, Pallas kernels, per_device(): pl.pallas_call(conv_kernel, grid=(GROUPS,), in_specs=[columns(raw_len, WI...  16.2 us
    unnamed x52, local copies, waits for them, and re-layouts  13.5 us
    dot_general x1, matrix products, per_device(): raw_near = jnp.dot(near_rows, near_half, preferred_element_type=jnp.float32)  13.2 us
    dot_general x1, matrix products, per_device(): raw_far = jnp.dot(far_rows, far_half, preferred_element_type=jnp.float32)  12.4 us
  transfers between devices with their start and end apart: 7, of which 5 were waited for; matrix products, arithmetic and copies ran while one was open for 4% of the time, Pallas kernels for 3%

profile of v3, /device:TPU:0, one launch (start us, length us, event | category | flops | bytes accessed | tf_op | source)
XLA Modules:
  0.0 440.5 jit_solution(13647857579886912578)
XLA Ops:
  6.5 1.2 constant_dynamic-slice_fusion
  7.7 0.5 collective-permute-start.1
  8.2 1.3 collective-permute-done.1
  9.5 1.1 broadcast_select_fusion.1
  10.6 0.9 pad_maximum_fusion.1
  11.5 135.0 %all-gather.4.cloned.1.call-done = bf16[1024,5120]{0,1:T(8,128)(2,1)} async-done(((bf16[1024,320]{0,1:T(8,128)(2,1)}), bf16[1024,5120]{0,1:T(8,128)(2,1)}) %all-gather.4.cloned.1.call-update) | async-done | bytes 10485776 | tf_op jit(solution)/shard_map/all_gather | solution.py:181
  146.5 0.1 select_reduce_fusion
  146.6 2.0 gather_fusion
  148.6 3.7 all-to-all-start
  152.4 0.1 pad_dynamic-slice_fusion.6
  152.6 0.6 slice.81
  153.2 0.6 slice.101
  153.9 1.3 pad_add_fusion
  155.2 0.2 slice_reduce_fusion.2
  155.3 1.4 compare_reduce_fusion
  156.9 44.5 %all-to-all-done = bf16[8,64,2048]{2,1,0:T(8,128)(2,1)S(1)} async-done(((bf16[8,64,2048]{2,1,0:T(8,128)(2,1)}), bf16[8,64,2048]{2,1,0:T(8,128)(2,1)S(1)}, u32[]{:S(2)}, u32[]{:S(2)}) %all-to-all-start) | async-done | bytes 2097184 | tf_op jit(solution)/shard_map/all_to_all | solution.py:166
  201.4 3.3 collective-permute-start
  204.7 0.8 negate_multiply_fusion
  205.6 1.2 reduce-window.6
  206.8 0.2 slice_reduce_fusion
  207.1 0.8 bitcast_bitcast_fusion
  207.8 0.2 slice_reduce_fusion.1
  208.0 0.8 exponential_select_fusion
  208.8 0.1 fusion.22
  208.9 0.3 copy.50.tail
  209.3 0.1 broadcast_in_dim.119
  209.4 0.1 squeeze.7
  209.6 0.1 broadcast_in_dim.123.through
  209.7 0.1 broadcast_in_dim.121.pass_last
  209.8 12.4 %fusion.13 = f32[528,5120]{1,0:T(8,128)} fusion(bf16[1024,5120]{0,1:T(8,128)(2,1)} %collective-permute-done.2, s32[]{:T(128)S(6)} %select_n.129, bf16[512,2048]{1,0:T(8,128)(2,1)S(1)} %bitcast.135, bf16[16,2048]{1,0:T(8,128)(2,1)S(1)} %collective-permute-done), kind=kOutput, calls=%fused_computation.28 | convolution fusion | flops 5538643968 | bytes 23461892 | tf_op jit(solution)/shard_map/dot_general | solution.py:188
  222.3 13.2 %add_convert_fusion.raw_x.raw_b.raw_c = bf16[528,5120]{1,0:T(8,128)(2,1)} fusion(f32[528,5120]{1,0:T(8,128)} %fusion.13, bf16[1024,5120]{0,1:T(8,128)(2,1)} %all-gather.4.cloned.1.call-done, s32[]{:T(128)S(6)} %select_n.127, bf16[512,2048]{1,0:T(8,128)(2,1)S(1)} %bitcast.136, bf16[16,2048]{1,0:T(8,128)(2,1)S(1)} %collective-permute-done), kind=kOutput, calls=%fused_computation.2 | convolution fusion | flops 5544050688 | bytes 28868612 | tf_op jit(solution)/shard_map/dot_general | solution.py:187
  235.5 0.3 broadcast_in_dim.113.match
  235.8 16.2 %shard_map.109 = (bf16[512,4096]{1,0:T(8,128)(2,1)S(1)}, bf16[512,512]{1,0:T(8,128)(2,1)S(1)}, bf16[512,512]{1,0:T(8,128)(2,1)S(1)}, f32[4,128,1024]{2,1,0:T(8,128)S(1)}, bf16[4,144,1024]{2,1,0:T(8,128)(2,1)S(1)}) custom-call(bf16[528,5120]{1,0:T(8,128)(2,1)} %add_convert_fusion.raw_x.raw_b.raw_c, bf16[528,5120]{1,0:T(8,128)(2,1)} %add_convert_fusion.raw_x.raw_b.raw_c, ...), custom_call_target="tpu_custom_call" | custom-call | flops 536870912 | bytes 14680064 | tf_op jit(solution)/shard_map/pallas_call | solution.py:239
  252.0 2.0 copy-done.3
  254.0 1.1 copy-done.8
  255.1 0.8 copy-done.14
  255.9 0.1 copy.54.seg_col
  256.2 0.1 broadcast_in_dim_reshape.3.skip
  256.3 1.2 copy.51
  257.5 0.1 broadcast_in_dim.129
  257.6 0.1 reshape_reshape.8
  257.7 1.3 copy.52
  259.1 0.7 copy.61
  259.7 0.1 copy.55
  259.8 0.1 reshape_reshape.9
  260.0 0.3 copy.56.factor
  260.3 1.0 compare_select_fusion
  261.3 2.5 copy-done.4
  263.9 1.2 copy-done.9
  265.1 0.9 copy-done.12
  266.0 1.0 copy-done.15
  267.0 11.4 %shard_map.110.inside = f32[512,4096]{1,0:T(8,128)} custom-call(bf16[512,4096]{1,0:T(8,128)(2,1)S(1)} %copy-done.4, bf16[512,512]{1,0:T(8,128)(2,1)S(1)} %copy-done.15, bf16[512,512]{1,0:T(8,128)(2,1)S(1)} %get-tuple-element.12.c_ref, f32[4,512,16]{2,1,0:T(8,128)S(1)} %bitcast.121, f32[4,16,512]{2,1,0:T(8,128)S(1)} %bitcast.125, ...), custom_call_target="tpu_custom_call" | custom-call | flops 8589934592 | bytes 14680064 | tf_op jit(solution)/shard_map/pallas_call | solution.py:283
  278.4 32.7 %all-gather.6.cloned.1.call-done = bf16[16,144,1024]{2,1,0:T(8,128)(2,1)} async-done(((bf16[4,144,1024]{2,1,0:T(8,128)(2,1)}), bf16[16,144,1024]{2,1,0:T(8,128)(2,1)}) %all-gather.6.cloned.1.call-update) | async-done | bytes 4718608 | tf_op jit(solution)/shard_map/all_gather | solution.py:281
  311.1 1.1 convert_reduce_fusion
  312.3 2.7 fusion.2
  315.0 2.7 fusion.8
  317.6 0.6 subtract_convert_fusion.lower
  318.3 0.4 fusion.upper
  318.6 1.8 copy-done.5
  320.4 7.3 %shard_map.111 = bf16[512,4096]{1,0:T(8,128)(2,1)S(1)} custom-call(f32[512,4096]{1,0:T(8,128)} %shard_map.110.inside, bf16[512,4096]{1,0:T(8,128)(2,1)S(1)} %copy-done.5, bf16[512,512]{1,0:T(8,128)(2,1)S(1)} %get-tuple-element.12.c_ref, bf16[2,4,128,1024]{3,2,1,0:T(8,128)(2,1)S(1)} %fusion.upper, bf16[2,4,128,1024]{3,2,1,0:T(8,128)(2,1)S(1)} %subtract_convert_fusion.lower, ...), custom_call_target="tpu_custom_call" | custom-call | flops 1073741824 | bytes 23068672 | tf_op jit(solution)/shard_map/pallas_call | solution.py:320
  327.8 2.0 copy-done.2
  329.8 4.6 %all-to-all-start.1 = ((bf16[8,64,4096]{2,1,0:T(8,128)(2,1)}), bf16[8,64,4096]{2,1,0:T(8,128)(2,1)}, u32[]{:S(2)}, u32[]{:S(2)}) async-start(bf16[8,64,4096]{2,1,0:T(8,128)(2,1)} %bitcast.120), calls=%async_computation.1 | async-start | bytes 8388608 | tf_op jit(solution)/shard_map/all_to_all | solution.py:345
  334.4 94.1 %all-to-all-done.1 = bf16[8,64,4096]{2,1,0:T(8,128)(2,1)} async-done(((bf16[8,64,4096]{2,1,0:T(8,128)(2,1)}), bf16[8,64,4096]{2,1,0:T(8,128)(2,1)}, u32[]{:S(2)}, u32[]{:S(2)}) %all-to-all-start.1) | async-done | bytes 4194336 | tf_op jit(solution)/shard_map/all_to_all | solution.py:345
  428.5 5.2 %gather_fusion.1 = bf16[8,64,4096]{2,1,0:T(8,128)(2,1)} fusion(bf16[8,64,4096]{2,1,0:T(8,128)(2,1)} %all-to-all-done.1, s32[1024]{0:T(1024)S(1)} %pad_clamp_fusion), kind=kCustom, calls=%fused_computation.1 | custom fusion | bytes 8388640 | tf_op jit(solution)/shard_map/jit(_take)/gather | solution.py:348
  (80 shorter events, 1.1 us)
Async XLA Ops:
  6.5 140.1 %copy-start = (bf16[512,2048]{1,0:T(8,128)(2,1)S(1)}, bf16[512,2048]{1,0:T(8,128)(2,1)}, u32[]{:S(2)}) copy-start(bf16[512,2048]{1,0:T(8,128)(2,1)} %param.11) | copy-start | bytes 6291460
  6.5 139.9 %copy-start.25 = (s32[1,8]{1,0:T(1,128)S(1)}, s32[1,8]{1,0:T(1,128)}, u32[]{:S(2)}) copy-start(s32[1,8]{1,0:T(1,128)} %param.21) | copy-start | bytes 100
  6.5 139.9 %all-gather.4.cloned.1.call-start = ((), (), s32[]{:S(2)}) async-start(), calls=%async_computation.2 | async-start | bytes 11141120 | tf_op jit(solution)/shard_map/all_gather | solution.py:181
  7.7 1.8 collective-permute-start.1
  146.5 63.4 %collective-permute-start.2 = (bf16[1024,5120]{0,1:T(8,128)(2,1)}, bf16[1024,5120]{0,1:T(8,128)(2,1)}, u32[]{:S(2)}, u32[]{:S(2)}) collective-permute-start(bf16[1024,5120]{0,1:T(8,128)(2,1)} %all-gather.4.cloned.1.call-done), channel_id=1, source_target_pairs={{0,1},{1,0},{2,3},{3,2},{4,5},{5,4},{6,7},{7,6},{8,9},{9,8},{10,11... | collective-permute-start | bytes 31457288 | tf_op jit(solution)/shard_map/ppermute | solution.py:184
  148.6 3.8 copy-start.21
  148.6 56.1 %copy-start.20 = (bf16[2048,64]{0,1:T(8,128)(2,1)S(1)}, bf16[2048,64]{0,1:T(8,128)(2,1)}, u32[]{:S(2)}) copy-start(bf16[2048,64]{0,1:T(8,128)(2,1)} %param.13) | copy-start | bytes 786436
  148.6 56.1 %copy-start.22 = (f32[64]{0:T(128)S(1)}, f32[64]{0:T(128)}, u32[]{:S(2)}) copy-start(f32[64]{0:T(128)} %param.17) | copy-start | bytes 772
  148.6 56.1 %copy-start.23 = (f32[64]{0:T(128)S(1)}, f32[64]{0:T(128)}, u32[]{:S(2)}) copy-start(f32[64]{0:T(128)} %param.16) | copy-start | bytes 772
  148.6 52.7 %all-to-all-start = ((bf16[8,64,2048]{2,1,0:T(8,128)(2,1)}), bf16[8,64,2048]{2,1,0:T(8,128)(2,1)S(1)}, u32[]{:S(2)}, u32[]{:S(2)}) async-start(bf16[8,64,2048]{2,1,0:T(8,128)(2,1)} %gather_fusion), calls=%async_computation | async-start | bytes 4194304 | tf_op jit(solution)/shard_map/all_to_all | solution.py:166
  152.4 158.7 %all-gather.6.cloned.1.call-start = ((), (), s32[]{:S(2)}) async-start(), calls=%async_computation.3 | async-start | bytes 5898240 | tf_op jit(solution)/shard_map/all_gather | solution.py:281
  201.4 8.5 %collective-permute-start = (bf16[16,2048]{1,0:T(8,128)(2,1)S(1)}, bf16[16,2048]{1,0:T(8,128)(2,1)S(1)}, u32[]{:S(2)}, u32[]{:S(2)}) collective-permute-start(bf16[16,2048]{1,0:T(8,128)(2,1)S(1)} %slice.96), channel_id=1, source_target_pairs={{0,8},{8,16},{16,24},{1,9},{9,17},{17,25},{2,10},{10,18},{18,26},{... | collective-permute-start | bytes 196616 | tf_op jit(solution)/shard_map/ppermute | solution.py:23
  205.6 3.3 copy-start.16
  207.8 1.1 copy-start.17
  222.3 13.5 %copy-start.10 = (f32[4,5120]{1,0:T(4,128)S(1)}, f32[4,5120]{1,0:T(4,128)}, u32[]{:S(2)}) copy-start(f32[4,5120]{1,0:T(4,128)} %w_c.1) | copy-start | bytes 245764
  222.3 13.5 %copy-start.11 = (f32[5120]{0:T(1024)S(1)}, f32[5120]{0:T(1024)}, u32[]{:S(2)}) copy-start(f32[5120]{0:T(1024)} %param.15) | copy-start | bytes 61444
  235.8 20.3 %copy-start.24 = (f32[64]{0:T(128)S(1)}, f32[64]{0:T(128)}, u32[]{:S(2)}) copy-start(f32[64]{0:T(128)} %param.18) | copy-start | bytes 772
  252.0 2.0 copy-start.3
  254.0 1.1 copy-start.8
  255.1 0.8 copy-start.14
  255.9 4.1 copy-start.6
  255.9 3.2 copy-start.18
  255.9 3.8 copy-start.19
  261.3 2.6 copy-start.4
  263.9 1.2 copy-start.9
  265.1 0.9 copy-start.12
  266.0 1.0 copy-start.15
  312.2 2.7 copy-start.7
  318.2 2.2 copy-start.5
  318.2 2.2 copy-start.13
  327.8 2.0 copy-start.2
  329.8 98.7 %all-to-all-start.1 = ((bf16[8,64,4096]{2,1,0:T(8,128)(2,1)}), bf16[8,64,4096]{2,1,0:T(8,128)(2,1)}, u32[]{:S(2)}, u32[]{:S(2)}) async-start(bf16[8,64,4096]{2,1,0:T(8,128)(2,1)} %bitcast.120), calls=%async_computation.1 | async-start | bytes 8388608 | tf_op jit(solution)/shard_map/all_to_all | solution.py:345
  428.5 5.2 %copy-start.1 = (bf16[512,2048]{1,0:T(8,128)(2,1)S(1)}, bf16[512,2048]{1,0:T(8,128)(2,1)}, u32[]{:S(2)}) copy-start(bf16[512,2048]{1,0:T(8,128)(2,1)} %param.11) | copy-start | bytes 6291460
Sparse Core Ops, SparseCore 0:
  11.6 134.7 all-gather.3
  256.0 55.0 all-gather.5

commit v4 on v3

--- a/solution.py
+++ b/solution.py
@@ -167,26 +167,10 @@
     tokens = tokens.reshape(tok_rows, stream_tokens.shape[1])
     prev_tokens = shifted(tokens[tok_rows - HALO :], "seq", 1)
     all_rows = jnp.concatenate([prev_tokens, tokens], axis=0)
-    depth = xbc_weight.shape[0] // 2
-    core = lax.rem(lax.axis_index("req"), 2)
-    swap = [(i, i ^ 1) for i in range(req_count)]
-    mine = lax.dynamic_slice_in_dim(xbc_weight, core * depth, depth, axis=0)
-    given = lax.dynamic_slice_in_dim(xbc_weight, (1 - core) * depth, depth, axis=0)
-    taken = lax.ppermute(given, "req", swap)
-    chip_half = jnp.concatenate(
-        [jnp.where(core == 0, mine, taken), jnp.where(core == 0, taken, mine)], axis=1
-    )
-    device_count = seq_count * req_count
-    same_core = [list(range(first, device_count, 2)) for first in range(2)]
-    near_half = lax.all_gather(
-        chip_half, ("seq", "req"), axis=1, tiled=True, axis_index_groups=same_core
-    )
-    far_half = lax.ppermute(near_half, "req", swap)
-    near_rows = lax.dynamic_slice_in_dim(all_rows, core * depth, depth, axis=1)
-    far_rows = lax.dynamic_slice_in_dim(all_rows, (1 - core) * depth, depth, axis=1)
-    raw_near = jnp.dot(near_rows, near_half, preferred_element_type=jnp.float32)
-    raw_far = jnp.dot(far_rows, far_half, preferred_element_type=jnp.float32)
-    raw_all = (raw_near + raw_far).astype(jnp.bfloat16)
+    full_weight = lax.all_gather(xbc_weight, ("seq", "req"), axis=1, tiled=True)
+    raw_all = jnp.dot(all_rows, full_weight, preferred_element_type=jnp.float32).astype(
+        jnp.bfloat16
+    )
     step_raw = jnp.dot(tokens, step_weight, preferred_element_type=jnp.float32).astype(jnp.bfloat16)
 
     seq_at = lax.axis_index("seq")
@@ -278,7 +262,7 @@
         raw_all, raw_all, raw_all, conv_weight, conv_weight, conv_weight,
         bias_row, bias_row, bias_row, match, tail, passing[1], through, expand,
     )
-    all_states = lax.all_gather(last_state, "seq")
+    earlier = [shifted(last_state, "seq", by) for by in range(1, seq_count)]
 
     inside = pl.pallas_call(
         mix_kernel,
@@ -304,13 +288,12 @@
         ),
     )(x_all, b_all, c_all, decay_col, decay_row, step_row, seg_rows[:, None], seg_rows[None, :])
 
-    all_through = jnp.sum(all_states[:, :, STATE : STATE + 3].astype(jnp.float32), axis=2, keepdims=True)
     running = jnp.ones((GROUPS, 1, WIDE), jnp.float32)
     incoming = jnp.zeros((GROUPS, STATE, WIDE), jnp.float32)
-    for turn in range(seq_count - 2, -1, -1):
-        share = jnp.where(turn < seq_at, running, 0.0)
-        incoming = incoming + share * all_states[turn, :, :STATE].astype(jnp.float32)
-        running = jnp.where(turn < seq_at, running * all_through[turn], running)
+    for arrived in earlier:
+        incoming = incoming + running * arrived[:, :STATE].astype(jnp.float32)
+        decays = arrived[:, STATE : STATE + 3].astype(jnp.float32)
+        running = running * jnp.sum(decays, axis=1, keepdims=True)
     states = jnp.stack([incoming, passing[0] * incoming + first_state])
     upper = states.astype(jnp.bfloat16)
     lower = (states - upper.astype(jnp.float32)).astype(jnp.bfloat16)

time: 441 us -> 398 us (0.902)
  waiting for transfers between devices: 308 us -> 262 us
  starting transfers between devices: 12.2 us -> 23.7 us
  matrix products: 26.5 us -> 18 us
    all_gather x2 -> x1, waiting for transfers between devices: 168 us -> 61.4 us  [per_device(): full_weight = lax.all_gather(xbc_weight, ('seq', 'req'), axis=1, tiled=True)]
    all_to_all x1, waiting for transfers between devices: 44.5 us -> 82 us  [per_device(): lax.all_to_all(outgoing, 'req', split_axis=0, concat_axis=0, tiled=True)]
    ppermute x1 -> x4, waiting for transfers between devices: 0.01 us -> 24.2 us  [shifted(): return lax.ppermute(shard, axis, pairs)]
    ppermute x1 -> x4, starting transfers between devices: 3.34 us -> 12.5 us  [shifted(): return lax.ppermute(shard, axis, pairs)]
    dot_general x2 -> x1, matrix products: 25.7 us -> 17.1 us  [per_device(): jnp.dot(all_rows, full_weight, preferred_element_type=jnp.float32)]
    unnamed x52 -> x66, local copies, waits for them, and re-layouts: 13.5 us -> 13.2 us
  transfers between devices with their start and end apart: 7 -> 7, of which waited for: 5 -> 4; matrix products, arithmetic and copies ran while one was open for 4% -> 6% of each run, Pallas kernels for 3% -> 3%
where the time goes in v4:
time: 398 us; the launch traced here: 397 us
  waiting for transfers between devices  262 us (66%)
  Pallas kernels  35.5 us (9%)
  local copies, waits for them, and re-layouts  30.5 us (8%)
  starting transfers between devices  23.7 us (6%)
  matrix products  18 us (5%)
  between operations  13.7 us (3%)
  other arithmetic  13.4 us (3%)
    all_to_all x1, waiting for transfers between devices, per_device(): lax.all_to_all(normed.reshape(req_count, page_rows, INNER), 'req', split_...  94 us
    all_to_all x1, waiting for transfers between devices, per_device(): lax.all_to_all(outgoing, 'req', split_axis=0, concat_axis=0, tiled=True)  82 us
    all_gather x1, waiting for transfers between devices, per_device(): full_weight = lax.all_gather(xbc_weight, ('seq', 'req'), axis=1, tiled=True)  61.4 us
    ppermute x4, waiting for transfers between devices, shifted(): return lax.ppermute(shard, axis, pairs)  24.2 us
    dot_general x1, matrix products, per_device(): jnp.dot(all_rows, full_weight, preferred_element_type=jnp.float32)  17.1 us
    pallas_call x1, Pallas kernels, per_device(): pl.pallas_call(conv_kernel, grid=(GROUPS,), in_specs=[columns(raw_len, WI...  16.8 us
    unnamed x66, local copies, waits for them, and re-layouts  13.2 us
    ppermute x4, starting transfers between devices, shifted(): return lax.ppermute(shard, axis, pairs)  12.5 us
  transfers between devices with their start and end apart: 7, of which 4 were waited for; matrix products, arithmetic and copies ran while one was open for 6% of the time, Pallas kernels for 3%

profile of v4, /device:TPU:0, one launch (start us, length us, event | category | flops | bytes accessed | tf_op | source)
XLA Modules:
  0.0 397.0 jit_solution(2101416897039319472)
XLA Ops:
  6.5 0.7 all-gather.2.cloned.1.call-update
  7.3 0.8 select_reduce_fusion
  8.0 0.1 copy-done
  8.1 2.0 gather_fusion
  10.1 6.5 %all-to-all-start = ((bf16[8,64,2048]{2,1,0:T(8,128)(2,1)}), bf16[8,64,2048]{2,1,0:T(8,128)(2,1)S(1)}, u32[]{:S(2)}, u32[]{:S(2)}) async-start(bf16[8,64,2048]{2,1,0:T(8,128)(2,1)} %gather_fusion), calls=%async_computation | async-start | bytes 4194304 | tf_op jit(solution)/shard_map/all_to_all | solution.py:166
  16.8 0.6 slice.76
  17.5 0.6 slice.95
  18.1 0.1 copy.54.seg_col
  18.3 0.7 broadcast_in_dim_reshape.3.skip
  19.0 1.3 pad_add_fusion
  20.3 0.2 slice_reduce_fusion.2
  20.5 1.4 compare_reduce_fusion
  21.8 0.6 add_convert_fusion
  22.6 82.0 %all-to-all-done = bf16[8,64,2048]{2,1,0:T(8,128)(2,1)S(1)} async-done(((bf16[8,64,2048]{2,1,0:T(8,128)(2,1)}), bf16[8,64,2048]{2,1,0:T(8,128)(2,1)S(1)}, u32[]{:S(2)}, u32[]{:S(2)}) %all-to-all-start) | async-done | bytes 2097184 | tf_op jit(solution)/shard_map/all_to_all | solution.py:166
  104.6 0.6 slice.90
  105.2 4.0 collective-permute-start
  109.2 0.8 negate_multiply_fusion
  110.1 1.2 reduce-window.6
  111.3 0.2 slice_reduce_fusion
  111.5 0.8 bitcast_bitcast_fusion
  112.3 0.2 slice_reduce_fusion.1
  112.4 0.1 exponential_select_fusion
  112.7 0.3 copy.50.tail
  113.3 0.7 broadcast_in_dim.113.pass_last
  114.0 0.6 copy-done.26
  114.7 0.7 broadcast_in_dim.115.through
  115.4 0.1 copy.55
  115.5 0.8 reshape_reshape.9
  116.3 61.4 %all-gather.2.cloned.1.call-done = bf16[2048,5120]{0,1:T(8,128)(2,1)} async-done(((bf16[2048,160]{0,1:T(8,128)(2,1)}), bf16[2048,5120]{0,1:T(8,128)(2,1)}) %all-gather.2.cloned.1.call-update) | async-done | bytes 20971536 | tf_op jit(solution)/shard_map/all_gather | solution.py:170
  177.7 17.1 %convolution_convert_fusion.raw_x.raw_b.raw_c = bf16[528,5120]{1,0:T(8,128)(2,1)} fusion(bf16[2048,5120]{0,1:T(8,128)(2,1)} %all-gather.2.cloned.1.call-done, bf16[512,2048]{1,0:T(8,128)(2,1)S(1)} %bitcast.100, bf16[16,2048]{1,0:T(8,128)(2,1)} %collective-permute-done), kind=kOutput, calls=%fused_computation.2 | convolution fusion | flops 11079991296 | bytes 28540928 | tf_op jit(solution)/shard_map/dot_general | solution.py:171
  194.8 0.3 broadcast_in_dim.105.match
  195.1 0.7 copy-done.9
  195.8 0.7 copy-done.11
  196.5 0.7 copy-done.12
  197.2 16.8 %shard_map.109 = (bf16[512,4096]{1,0:T(8,128)(2,1)S(1)}, bf16[512,512]{1,0:T(8,128)(2,1)S(1)}, bf16[512,512]{1,0:T(8,128)(2,1)S(1)}, f32[4,128,1024]{2,1,0:T(8,128)S(1)}, bf16[4,144,1024]{2,1,0:T(8,128)(2,1)}) custom-call(bf16[528,5120]{1,0:T(8,128)(2,1)} %convolution_convert_fusion.raw_x.raw_b.raw_c, ...), custom_call_target="tpu_custom_call" | custom-call | flops 536870912 | bytes 14680064 | tf_op jit(solution)/shard_map/pallas_call | solution.py:223
  214.1 2.0 copy-done.3
  216.1 0.8 copy-done.17
  216.9 4.5 %collective-permute-start.1 = (bf16[4,144,1024]{2,1,0:T(8,128)(2,1)}, bf16[4,144,1024]{2,1,0:T(8,128)(2,1)}, u32[]{:S(2)}, u32[]{:S(2)}) collective-permute-start(bf16[4,144,1024]{2,1,0:T(8,128)(2,1)} %get-tuple-element.13), channel_id=1, source_target_pairs={{0,8},{8,16},{16,24},{1,9},{9,17},{17,25},{2,10},{10,18},{18,26},{... | collective-permute-start | bytes 3538952 | tf_op jit(solution)/shard_map/ppermute | solution.py:23
  221.4 2.5 collective-permute-start.2
  223.9 0.7 pad_maximum_fusion.2
  224.6 0.1 copy.51
  224.7 0.1 reshape_reshape.8
  224.8 1.3 copy.52
  226.1 0.7 copy.61
  227.0 1.2 copy.56.factor
  228.1 1.5 collective-permute-start.3
  229.7 1.0 compare_select_fusion
  230.7 2.2 copy-done.4
  232.9 1.2 copy-done.7
  234.1 0.9 copy-done.10
  235.0 1.0 copy-done.18
  236.1 11.4 %shard_map.110.inside = f32[512,4096]{1,0:T(8,128)} custom-call(bf16[512,4096]{1,0:T(8,128)(2,1)S(1)} %copy-done.4, bf16[512,512]{1,0:T(8,128)(2,1)S(1)} %copy-done.18, bf16[512,512]{1,0:T(8,128)(2,1)S(1)} %get-tuple-element.12.c_ref, f32[4,512,16]{2,1,0:T(8,128)S(1)} %bitcast.89, f32[4,16,512]{2,1,0:T(8,128)S(1)} %bitcast.93, f32[4,16,512]{2,1,0:T(8,128)S(1)} %bitcast.94, ...), custom_call_target="tpu_custom_call" | custom-call | flops 8589934592 | bytes 14680064 | tf_op jit(solution)/shard_map/pallas_call | solution.py:267
  247.4 0.9 convert_reduce_fusion.1
  248.3 24.2 %collective-permute-done.2 = bf16[4,144,1024]{2,1,0:T(8,128)(2,1)} collective-permute-done((bf16[4,144,1024]{2,1,0:T(8,128)(2,1)}, bf16[4,144,1024]{2,1,0:T(8,128)(2,1)}, u32[]{:S(2)}, u32[]{:S(2)}) %collective-permute-start.2) | collective-permute-done | bytes 1179680 | tf_op jit(solution)/shard_map/ppermute | solution.py:23
  272.5 0.9 convert_reduce_fusion
  273.4 2.4 fusion.6
  275.8 0.4 fusion.upper
  276.2 0.6 subtract_convert_fusion.lower
  276.8 0.1 copy-done.13
  277.0 7.3 %shard_map.111 = bf16[512,4096]{1,0:T(8,128)(2,1)S(1)} custom-call(f32[512,4096]{1,0:T(8,128)} %shard_map.110.inside, bf16[512,4096]{1,0:T(8,128)(2,1)S(1)} %copy-done.4, bf16[512,512]{1,0:T(8,128)(2,1)S(1)} %get-tuple-element.12.c_ref, bf16[2,4,128,1024]{3,2,1,0:T(8,128)(2,1)S(1)} %fusion.upper, bf16[2,4,128,1024]{3,2,1,0:T(8,128)(2,1)S(1)} %subtract_convert_fusion.lower, ...), custom_call_target="tpu_custom_call" | custom-call | flops 1073741824 | bytes 23068672 | tf_op jit(solution)/shard_map/pallas_call | solution.py:303
  284.3 2.0 copy-done.2
  286.3 4.7 %all-to-all-start.1 = ((bf16[8,64,4096]{2,1,0:T(8,128)(2,1)}), bf16[8,64,4096]{2,1,0:T(8,128)(2,1)}, u32[]{:S(2)}, u32[]{:S(2)}) async-start(bf16[8,64,4096]{2,1,0:T(8,128)(2,1)} %bitcast.88), calls=%async_computation.1 | async-start | bytes 8388608 | tf_op jit(solution)/shard_map/all_to_all | solution.py:328
  291.0 94.0 %all-to-all-done.1 = bf16[8,64,4096]{2,1,0:T(8,128)(2,1)} async-done(((bf16[8,64,4096]{2,1,0:T(8,128)(2,1)}), bf16[8,64,4096]{2,1,0:T(8,128)(2,1)}, u32[]{:S(2)}, u32[]{:S(2)}) %all-to-all-start.1) | async-done | bytes 4194336 | tf_op jit(solution)/shard_map/all_to_all | solution.py:328
  385.0 5.2 %gather_fusion.1 = bf16[8,64,4096]{2,1,0:T(8,128)(2,1)} fusion(bf16[8,64,4096]{2,1,0:T(8,128)(2,1)} %all-to-all-done.1, s32[1024]{0:T(1024)S(1)} %pad_clamp_fusion), kind=kCustom, calls=%fused_computation.1 | custom fusion | bytes 8388640 | tf_op jit(solution)/shard_map/jit(_take)/gather | solution.py:331
  (89 shorter events, 1.4 us)
Async XLA Ops:
  6.5 1.6 copy-start
  6.5 171.1 %all-gather.2.cloned.1.call-start = ((), (), s32[]{:S(2)}) async-start(), calls=%async_computation.2 | async-start | bytes 21626880 | tf_op jit(solution)/shard_map/all_gather | solution.py:170
  10.1 6.5 %copy-start.28 = (s32[1,2048]{1,0:T(1,128)S(1)}, s32[1,2048]{1,0:T(1,128)}, u32[]{:S(2)}) copy-start(s32[1,2048]{1,0:T(1,128)} %param.20) | copy-start | bytes 24580
  10.1 8.1 %copy-start.29 = (f32[64]{0:T(128)S(1)}, f32[64]{0:T(128)}, u32[]{:S(2)}) copy-start(f32[64]{0:T(128)} %param.18) | copy-start | bytes 772
  10.1 99.0 %copy-start.24 = (bf16[2048,64]{0,1:T(8,128)(2,1)S(1)}, bf16[2048,64]{0,1:T(8,128)(2,1)}, u32[]{:S(2)}) copy-start(bf16[2048,64]{0,1:T(8,128)(2,1)} %param.13) | copy-start | bytes 786436
  10.1 99.0 %copy-start.30 = (f32[64]{0:T(128)S(1)}, f32[64]{0:T(128)}, u32[]{:S(2)}) copy-start(f32[64]{0:T(128)} %param.17) | copy-start | bytes 772
  10.1 99.0 %copy-start.31 = (f32[64]{0:T(128)S(1)}, f32[64]{0:T(128)}, u32[]{:S(2)}) copy-start(f32[64]{0:T(128)} %param.16) | copy-start | bytes 772
  10.1 94.4 %all-to-all-start = ((bf16[8,64,2048]{2,1,0:T(8,128)(2,1)}), bf16[8,64,2048]{2,1,0:T(8,128)(2,1)S(1)}, u32[]{:S(2)}, u32[]{:S(2)}) async-start(bf16[8,64,2048]{2,1,0:T(8,128)(2,1)} %gather_fusion), calls=%async_computation | async-start | bytes 4194304 | tf_op jit(solution)/shard_map/all_to_all | solution.py:166
  16.8 95.5 %copy-start.14 = (s32[512]{0:T(512)}, s32[512]{0:T(512)S(1)}, u32[]{:S(2)}) copy-start(s32[512]{0:T(512)S(1)} %slice.68) | copy-start | bytes 6148
  105.2 11.1 %collective-permute-start = (bf16[16,2048]{1,0:T(8,128)(2,1)}, bf16[16,2048]{1,0:T(8,128)(2,1)}, u32[]{:S(2)}, u32[]{:S(2)}) collective-permute-start(bf16[16,2048]{1,0:T(8,128)(2,1)} %slice.90), channel_id=1, source_target_pairs={{0,8},{8,16},{16,24},{1,9},{9,17},{17,25},{2,10},{10,18},{18,26},{... | collective-permute-start | bytes 196616 | tf_op jit(solution)/shard_map/ppermute | solution.py:23
  110.0 84.8 %copy-start.19 = (f32[512,64]{0,1:T(8,128)}, f32[512,64]{0,1:T(8,128)S(1)}, u32[]{:S(2)}) copy-start(f32[512,64]{0,1:T(8,128)S(1)} %get-tuple-element.33) | copy-start | bytes 393220
  112.3 82.5 %copy-start.20 = (f32[2,256,64]{1,2,0:T(8,128)}, f32[2,256,64]{1,2,0:T(8,128)S(1)}, u32[]{:S(2)}) copy-start(f32[2,256,64]{1,2,0:T(8,128)S(1)} %get-tuple-element.26) | copy-start | bytes 393220
  114.0 0.6 copy-start.26
  116.3 78.5 %copy-start.25 = (f32[3,512]{1,0:T(4,128)S(1)}, f32[3,512]{1,0:T(4,128)}, u32[]{:S(2)}) copy-start(f32[3,512]{1,0:T(4,128)} %add_convert_fusion) | copy-start | bytes 18436
  116.3 78.8 %copy-start.8 = (f32[4,5120]{1,0:T(4,128)S(1)}, f32[4,5120]{1,0:T(4,128)}, u32[]{:S(2)}) copy-start(f32[4,5120]{1,0:T(4,128)} %w_c.1) | copy-start | bytes 245764
  195.1 0.7 copy-start.9
  195.8 0.7 copy-start.11
  196.5 0.7 copy-start.12
  197.2 24.2 %copy-start.23 = (f32[512,4,16]{0,2,1:T(8,128)S(1)}, f32[512,4,16]{0,2,1:T(8,128)}, u32[]{:S(2)}) copy-start(f32[512,4,16]{0,2,1:T(8,128)} %reshape_reshape.9) | copy-start | bytes 393220
  197.2 27.3 %copy-start.21 = (f32[2,256,64]{1,2,0:T(8,128)S(1)}, f32[2,256,64]{1,2,0:T(8,128)}, u32[]{:S(2)}) copy-start(f32[2,256,64]{1,2,0:T(8,128)} %copy-done.20) | copy-start | bytes 393220
  214.1 2.0 copy-start.3
  216.1 0.8 copy-start.17
  216.9 13.8 %copy-start.5 = (f32[4,128,1024]{2,1,0:T(8,128)}, f32[4,128,1024]{2,1,0:T(8,128)S(1)}, u32[]{:S(2)}) copy-start(f32[4,128,1024]{2,1,0:T(8,128)S(1)} %get-tuple-element.14) | copy-start | bytes 6291460
  216.9 9.2 %copy-start.22 = (f32[2,8,8,256]{3,2,1,0:T(8,128)S(1)}, f32[2,8,8,256]{3,2,1,0:T(8,128)}, u32[]{:S(2)}) copy-start(f32[2,8,8,256]{3,2,1,0:T(8,128)} %get-tuple-element.25) | copy-start | bytes 393220
  216.9 9.9 %copy-start.27 = (f32[4,16]{1,0:T(4,128)S(1)}, f32[4,16]{1,0:T(4,128)}, u32[]{:S(2)}) copy-start(f32[4,16]{1,0:T(4,128)} %copy-done.26) | copy-start | bytes 772
  216.9 13.8 %copy-start.15 = (s32[512]{0:T(512)S(1)}, s32[512]{0:T(512)}, u32[]{:S(2)}) copy-start(s32[512]{0:T(512)} %copy-done.14) | copy-start | bytes 6148
  216.9 30.5 %collective-permute-start.1 = (bf16[4,144,1024]{2,1,0:T(8,128)(2,1)}, bf16[4,144,1024]{2,1,0:T(8,128)(2,1)}, u32[]{:S(2)}, u32[]{:S(2)}) collective-permute-start(bf16[4,144,1024]{2,1,0:T(8,128)(2,1)} %get-tuple-element.13), channel_id=1, source_target_pairs={{0,8},{8,16},{16,24},{1,9},{9,17},{17,25},{2,10},{10,18},{18,26},{... | collective-permute-start | bytes 3538952 | tf_op jit(solution)/shard_map/ppermute | solution.py:23
  221.4 51.1 %collective-permute-start.2 = (bf16[4,144,1024]{2,1,0:T(8,128)(2,1)}, bf16[4,144,1024]{2,1,0:T(8,128)(2,1)}, u32[]{:S(2)}, u32[]{:S(2)}) collective-permute-start(bf16[4,144,1024]{2,1,0:T(8,128)(2,1)} %get-tuple-element.13), channel_id=1, source_target_pairs={{0,16},{8,24},{1,17},{9,25},{2,18},{10,26},{3,19},{11,27},{4,20},{... | collective-permute-start | bytes 3538952 | tf_op jit(solution)/shard_map/ppermute | solution.py:23
  228.1 45.3 %collective-permute-start.3 = (bf16[4,144,1024]{2,1,0:T(8,128)(2,1)}, bf16[4,144,1024]{2,1,0:T(8,128)(2,1)S(1)}, u32[]{:S(2)}, u32[]{:S(2)}) collective-permute-start(bf16[4,144,1024]{2,1,0:T(8,128)(2,1)} %get-tuple-element.13), channel_id=1, source_target_pairs={{0,24},{1,25},{2,26},{3,27},{4,28},{5,29},{6,30},{7,31}} | collective-permute-start | bytes 3538952 | tf_op jit(solution)/shard_map/ppermute | solution.py:23
  230.7 2.2 copy-start.4
  232.9 1.2 copy-start.7
  234.1 0.9 copy-start.10
  235.0 1.0 copy-start.18
  236.1 37.4 %copy-start.6 = (f32[4,128,1024]{2,1,0:T(8,128)S(1)}, f32[4,128,1024]{2,1,0:T(8,128)}, u32[]{:S(2)}) copy-start(f32[4,128,1024]{2,1,0:T(8,128)} %copy-done.5) | copy-start | bytes 6291460
  276.2 0.7 copy-start.13
  276.2 0.7 copy-start.16
  284.3 2.0 copy-start.2
  286.3 4.7 %copy-start.32 = (s32[1,8]{1,0:T(1,128)S(1)}, s32[1,8]{1,0:T(1,128)}, u32[]{:S(2)}) copy-start(s32[1,8]{1,0:T(1,128)} %param.21) | copy-start | bytes 100
  286.3 98.7 %all-to-all-start.1 = ((bf16[8,64,4096]{2,1,0:T(8,128)(2,1)}), bf16[8,64,4096]{2,1,0:T(8,128)(2,1)}, u32[]{:S(2)}, u32[]{:S(2)}) async-start(bf16[8,64,4096]{2,1,0:T(8,128)(2,1)} %bitcast.88), calls=%async_computation.1 | async-start | bytes 8388608 | tf_op jit(solution)/shard_map/all_to_all | solution.py:328
  385.0 5.2 %copy-start.1 = (bf16[512,2048]{1,0:T(8,128)(2,1)S(1)}, bf16[512,2048]{1,0:T(8,128)(2,1)}, u32[]{:S(2)}) copy-start(bf16[512,2048]{1,0:T(8,128)(2,1)} %param.11) | copy-start | bytes 6291460
Sparse Core Ops, SparseCore 0:
  10.2 167.4 all-gather.1
